TPU v7x, 512 devices: a whole 4x4x16 slice. The times are simulated.
512 devices in a mesh: row: 16 (over y_lo, x, core), col: 32 (over z, y_hi).
Axes of the slice: x: 4, y: 4 (y_hi: 2, y_lo: 2; y = y_hi * 2 + y_lo), z: 16, core: 2. Of those that a mesh axis runs over, the one named last changes fastest.
Arguments:
- specimen: float32 [2, 4096, 8192], P(None, 'row', 'col'), may hold values from -5 to 5
- probe_modes: bfloat16 [4, 2, 256, 256], replicated, may hold values from -5 to 5
- amplitude: float32 [16, 32, 1, 256, 256], P('row', 'col'), may hold values from 0.5 to 4
- offsets: int32 [16, 32, 1, 2], P('row', 'col'), may hold values from 0 to 7936, as said below
- counts: int32 [16, 32], P('row', 'col'), may hold values from 0 to 1, as said below
Outputs:
- specimen_grad: float32 [2, 4096, 8192], P(None, 'row', 'col')
- probe_grad: float32 [4, 2, 256, 256], P(None, None, 'row', 'col')
Inputs may be any that keep to these rules, and one draw needn't show every extreme that they name: offsets[a, b, s] = (r, c) satisfies a * 256 <= r < (a + 1) * 256, b * 256 <= c < (b + 1) * 256, r <= 3840 and c <= 7936: every patch lies inside the specimen and starts in its own tile. counts[a, b] is the number of live slots of tile (a, b); slots from counts[a, b] on carry drawn offsets and amplitudes that no output uses.
All inputs are finite; a program needn't handle non-finite values.
Results may differ from a plain program's by a relative error of at most 0.0079.
The roundings to bfloat16 on the way count: a program that leaves them out, or rounds other values in their place, can miss the bound.
Values sent between devices are 32-bit elements; how exact they have to be, the bound alone decides.
No kernel may reach another device: no remote copies, remote signals or barrier semaphores. Data moves between devices by JAX's collectives and lax.ppermute only.
A program may use at most 64 MiB of HBM per device.

v0:
```python
import math

import jax
import jax.numpy as jnp
from jax import lax
from jax.sharding import PartitionSpec as P


def shifted(value, axis, steps):
    count = lax.axis_size(axis)
    first, last = (max(0, -steps), min(count, count - steps))
    return lax.ppermute(value, axis, [(source, source + steps) for source in range(first, last)])


def dft_tables(length, imag_sign):
    sample_index = jnp.arange(length, dtype=jnp.int32)
    phase_angle = (sample_index[:, None] * sample_index[None, :] % length).astype(jnp.float32) * (
        2.0 * math.pi / length
    )
    factor = 1.0 / math.sqrt(length)
    real_part = (jnp.cos(phase_angle) * factor).astype(jnp.bfloat16)
    imag_part = (imag_sign * jnp.sin(phase_angle) * factor).astype(jnp.bfloat16)
    left_table = jnp.concatenate(
        [jnp.concatenate([real_part, -imag_part], 1), jnp.concatenate([imag_part, real_part], 1)], 0
    )
    right_table = jnp.stack(
        [jnp.stack([real_part, imag_part], 1), jnp.stack([-imag_part, real_part], 1)], 0
    )
    return (left_table, right_table)


def transform(fields, left_table, right_table):
    mode_count = fields.shape[0]
    length = fields.shape[2]
    stacked = fields.reshape(mode_count, 2 * length, length)
    midway = jnp.einsum(
        "xb,mbq->mxq", left_table, stacked, preferred_element_type=jnp.float32
    ).astype(jnp.bfloat16)
    midway = midway.reshape(mode_count, 2, length, length)
    return jnp.einsum("mrpq,rqst->mspt", midway, right_table, preferred_element_type=jnp.float32)


def slot_terms(patch_field, illumination, amplitude_slot, forward, inverse):
    real_exit = illumination[:, 0] * patch_field[0] - illumination[:, 1] * patch_field[1]
    imag_exit = illumination[:, 0] * patch_field[1] + illumination[:, 1] * patch_field[0]
    exit_wave = jnp.stack([real_exit, imag_exit], 1)
    far_field = transform(exit_wave.astype(jnp.bfloat16), forward[0], forward[1])
    modulus = jnp.sqrt(jnp.sum(far_field * far_field, axis=(0, 1)))
    rescale = amplitude_slot / jnp.maximum(modulus, 0.5)
    projected = transform((far_field * rescale).astype(jnp.bfloat16), inverse[0], inverse[1])
    residual_wave = exit_wave - projected
    spec_real = jnp.sum(
        illumination[:, 0] * residual_wave[:, 0] + illumination[:, 1] * residual_wave[:, 1], 0
    )
    spec_imag = jnp.sum(
        illumination[:, 0] * residual_wave[:, 1] - illumination[:, 1] * residual_wave[:, 0], 0
    )
    probe_real = patch_field[0] * residual_wave[:, 0] + patch_field[1] * residual_wave[:, 1]
    probe_imag = patch_field[0] * residual_wave[:, 1] - patch_field[1] * residual_wave[:, 0]
    return (jnp.stack([spec_real, spec_imag]), jnp.stack([probe_real, probe_imag], 1))


def shards(specimen, probe_modes, amplitude, offsets, counts):
    tile_rows = specimen.shape[1]
    tile_cols = specimen.shape[2]
    mode_count = probe_modes.shape[0]
    length = probe_modes.shape[2]
    slot_count = offsets.shape[2]
    below_rows = shifted(specimen, "row", -1)
    column_pair = jnp.concatenate([specimen, below_rows], 1)
    beside = shifted(column_pair, "col", -1)
    extended = jnp.concatenate([column_pair, beside], 2)
    band_start = lax.axis_index("row") * tile_rows
    tile_start = lax.axis_index("col") * tile_cols
    local_rows = offsets[0, 0, :, 0] - band_start
    local_cols = offsets[0, 0, :, 1] - tile_start
    live_count = counts[0, 0]
    forward = dft_tables(length, -1.0)
    inverse = dft_tables(length, 1.0)
    illumination = probe_modes.astype(jnp.float32)

    def one_slot(slot_index, running):
        spec_acc, probe_acc = running
        start_row = local_rows[slot_index]
        start_col = local_cols[slot_index]
        zero_index = jnp.zeros((), jnp.int32)
        patch_field = lax.dynamic_slice(
            extended, (zero_index, start_row, start_col), (2, length, length)
        )
        spec_term, probe_term = slot_terms(
            patch_field, illumination, amplitude[0, 0, slot_index], forward, inverse
        )
        weight = (slot_index < live_count).astype(jnp.float32)
        window_old = lax.dynamic_slice(
            spec_acc, (zero_index, start_row, start_col), (2, length, length)
        )
        spec_acc = lax.dynamic_update_slice(
            spec_acc, window_old + weight * spec_term, (zero_index, start_row, start_col)
        )
        return (spec_acc, probe_acc + weight * probe_term)

    start_state = (
        jnp.zeros((2, tile_rows + tile_rows, tile_cols + tile_cols), jnp.float32),
        jnp.zeros((mode_count, 2, length, length), jnp.float32),
    )
    spec_acc, probe_acc = lax.fori_loop(0, slot_count, one_slot, start_state)
    from_left = shifted(spec_acc[:, :, tile_cols:], "col", 1)
    merged = spec_acc[:, :, :tile_cols].at[:, :, :tile_cols].add(from_left)
    from_above = shifted(merged[:, tile_rows:, :], "row", 1)
    specimen_grad = merged[:, :tile_rows, :].at[:, :tile_rows, :].add(from_above)
    band_total = lax.axis_size("row")
    tile_total = lax.axis_size("col")
    inverse_slots = 1.0 / (band_total * tile_total * slot_count)
    summed = lax.psum(probe_acc, ("row", "col"))
    rows_part = length // band_total
    cols_part = length // tile_total
    zero_index = jnp.zeros((), jnp.int32)
    own_share = lax.dynamic_slice(
        summed,
        (
            zero_index,
            zero_index,
            lax.axis_index("row") * rows_part,
            lax.axis_index("col") * cols_part,
        ),
        (mode_count, 2, rows_part, cols_part),
    )
    probe_grad = own_share * inverse_slots
    return (specimen_grad, probe_grad)


def solution(mesh):
    in_specs = (
        P(None, "row", "col"),
        P(),
        P("row", "col", None, None, None),
        P("row", "col", None, None),
        P("row", "col"),
    )
    out_specs = (P(None, "row", "col"), P(None, None, "row", "col"))
    return jax.shard_map(shards, mesh=mesh, in_specs=in_specs, out_specs=out_specs, check_vma=False)
```

profile of v0, /device:TPU:1, one launch (start us, length us, event | category | flops | bytes accessed | tf_op | source)
XLA Modules:
  0.0 574.3 jit_solution(16899622633033783852)
XLA Ops:
  7.2 8.9 %collective-permute-start = (f32[2,256,256]{2,1,0:T(8,128)}, f32[2,256,256]{2,1,0:T(8,128)S(1)}, u32[]{:S(2)}, u32[]{:S(2)}) collective-permute-start(f32[2,256,256]{2,1,0:T(8,128)} %param.13), channel_id=1, source_target_pairs={{32,0},{64,32},{96,64},{128,96},{160,128},{192,160},{224,192},{256... | collective-permute-start | bytes 1572872 | tf_op jit(solution)/shard_map/ppermute | solution.py:12
  16.2 1.9 constant_dynamic-update-slice_fusion.1
  18.1 0.9 collective-permute-done
  18.9 0.9 constant_dynamic-update-slice_fusion
  19.8 1.3 collective-permute-start.1
  21.1 0.6 fusion.46
  23.0 0.5 copy.27
  23.5 0.2 convert_element_type.160
  24.4 1.6 fusion.41
  26.0 1.0 multiply_convert_fusion.5
  27.0 1.0 fusion.42
  28.0 1.6 multiply_convert_fusion
  29.6 1.8 multiply_convert_fusion.1
  31.4 1.0 multiply_convert_fusion.3
  32.4 1.0 fusion.39
  33.4 1.1 fusion.23
  34.5 13.7 %collective-permute-done.1 = f32[2,512,256]{2,1,0:T(8,128)} collective-permute-done((f32[2,512,256]{2,1,0:T(8,128)}, f32[2,512,256]{2,1,0:T(8,128)}, u32[]{:S(2)}, u32[]{:S(2)}) %collective-permute-start.1) | collective-permute-done | bytes 1048608 | tf_op jit(solution)/shard_map/ppermute | solution.py:12
  48.2 1.5 fusion.12
  49.7 0.1 copy.28
  49.9 0.8 copy.29
  50.7 1.2 multiply_subtract_fusion.1
  52.0 0.2 fusion.5
  52.3 0.7 copy-done
  53.0 0.2 copy-done.8
  53.2 0.2 copy-done.9
  53.4 1.7 fusion.3
  55.1 2.3 copy.46
  57.3 2.2 fusion
  59.5 0.1 bitcast_divide_fusion
  59.7 0.3 fusion.1
  60.0 0.5 copy-done.5
  60.6 1.7 fusion.4
  62.3 2.3 copy.47
  64.6 2.5 bitcast_subtract_fusion
  67.1 1.5 multiply_add_fusion
  68.7 1.0 copy.37
  69.7 0.2 broadcast_in_dim.3
  70.0 7.5 %dynamic_update_slice.4 = f32[2,512,512]{2,1,0:T(8,128)S(1)} dynamic-update-slice(f32[2,512,512]{2,1,0:T(8,128)S(1)} %broadcast_in_dim.3, f32[2,256,256]{2,1,0:T(8,128)} %copy.37, s32[]{:T(128)} %constant.114.clone.1, s32[]{:T(128)S(6)} %select_n.84, s32[]{:T(128)S(6)} %select_n.85) | dynamic-update-slice | bytes 1048580 | tf_op jit(solution)/shard_map/while/body/eval_jaxpr/dynamic_update_slice | solution.py:97
  77.5 1.1 slice.117
  78.6 2.9 collective-permute-start.2
  81.4 1.5 maximum_multiply_fusion
  83.0 18.4 %collective-permute-done.2 = f32[2,512,256]{2,1,0:T(8,128)} collective-permute-done((f32[2,512,256]{2,1,0:T(8,128)}, f32[2,512,256]{2,1,0:T(8,128)}, u32[]{:S(2)}, u32[]{:S(2)}) %collective-permute-start.2) | collective-permute-done | bytes 1048608 | tf_op jit(solution)/shard_map/ppermute | solution.py:12
  101.4 1.4 slice_add_fusion
  102.8 10.8 %collective-permute-start.3 = (f32[2,256,256]{2,1,0:T(8,128)S(1)}, f32[2,256,256]{2,1,0:T(8,128)S(1)}, u32[]{:S(2)}, u32[]{:S(2)}) collective-permute-start(f32[2,256,256]{2,1,0:T(8,128)S(1)} %slice.119), channel_id=1, source_target_pairs={{0,32},{32,64},{64,96},{96,128},{128,160},{160,192},{192,224},{224... | collective-permute-start | bytes 1572872 | tf_op jit(solution)/shard_map/ppermute | solution.py:12
  113.7 451.4 %all-reduce.2.cloned.1.call-done = f32[4,2,256,256]{2,3,0,1:T(8,128)} async-done(((f32[4,2,256,256]{2,3,0,1:T(8,128)}), f32[4,2,256,256]{2,3,0,1:T(8,128)}) %all-reduce.2.cloned.1.call-update) | async-done | bytes 2097168 | tf_op jit(solution)/shard_map/psum | solution.py:114
  565.1 0.8 dynamic-slice_multiply_fusion
  566.0 0.6 copy.38
  566.6 0.9 slice_add_fusion.1
  (26 shorter events, 0.5 us)
Async XLA Ops:
  7.2 13.9 %copy-start.10 = (s32[1,1,1,2]{3,2,1,0:T(1,128)S(1)}, s32[1,1,1,2]{3,2,1,0:T(1,128)}, u32[]{:S(2)}) copy-start(s32[1,1,1,2]{3,2,1,0:T(1,128)} %param.16) | copy-start | bytes 28
  7.2 15.8 %copy-start.3 = (bf16[4,2,256,256]{3,2,1,0:T(8,128)(2,1)S(1)}, bf16[4,2,256,256]{3,2,1,0:T(8,128)(2,1)}, u32[]{:S(2)}) copy-start(bf16[4,2,256,256]{3,2,1,0:T(8,128)(2,1)} %param.14) | copy-start | bytes 3145732
  7.2 558.0 %all-reduce.2.cloned.1.call-start = ((), (), s32[]{:S(2)}) async-start(), calls=%async_computation | async-start | bytes 4194304 | tf_op jit(solution)/shard_map/psum | solution.py:114
  7.2 11.7 %collective-permute-start = (f32[2,256,256]{2,1,0:T(8,128)}, f32[2,256,256]{2,1,0:T(8,128)S(1)}, u32[]{:S(2)}, u32[]{:S(2)}) collective-permute-start(f32[2,256,256]{2,1,0:T(8,128)} %param.13), channel_id=1, source_target_pairs={{32,0},{64,32},{96,64},{128,96},{160,128},{192,160},{224,192},{256... | collective-permute-start | bytes 1572872 | tf_op jit(solution)/shard_map/ppermute | solution.py:12
  19.8 28.4 %collective-permute-start.1 = (f32[2,512,256]{2,1,0:T(8,128)}, f32[2,512,256]{2,1,0:T(8,128)}, u32[]{:S(2)}, u32[]{:S(2)}) collective-permute-start(f32[2,512,256]{2,1,0:T(8,128)} %constant_dynamic-update-slice_fusion), channel_id=1, source_target_pairs={{1,0},{2,1},{3,2},{4,3},{5,4},{6,5},{7,6},{8,7},{9,8},{10,9},{11,1... | collective-permute-start | bytes 3145736 | tf_op jit(solution)/shard_map/ppermute | solution.py:12
  51.9 1.0 copy-start
  52.0 1.0 copy-start.6
  52.0 1.2 copy-start.8
  52.0 1.4 copy-start.9
  57.3 2.2 copy-start.4
  59.6 0.9 copy-start.5
  59.6 1.0 copy-start.7
  64.6 2.5 copy-start.2
  77.5 4.0 copy-start.1
  78.6 22.8 %collective-permute-start.2 = (f32[2,512,256]{2,1,0:T(8,128)}, f32[2,512,256]{2,1,0:T(8,128)}, u32[]{:S(2)}, u32[]{:S(2)}) collective-permute-start(f32[2,512,256]{2,1,0:T(8,128)} %slice.117), channel_id=1, source_target_pairs={{0,1},{1,2},{2,3},{3,4},{4,5},{5,6},{6,7},{7,8},{8,9},{9,10},{10,1... | collective-permute-start | bytes 3145736 | tf_op jit(solution)/shard_map/ppermute | solution.py:12
  102.8 463.8 %collective-permute-start.3 = (f32[2,256,256]{2,1,0:T(8,128)S(1)}, f32[2,256,256]{2,1,0:T(8,128)S(1)}, u32[]{:S(2)}, u32[]{:S(2)}) collective-permute-start(f32[2,256,256]{2,1,0:T(8,128)S(1)} %slice.119), channel_id=1, source_target_pairs={{0,32},{32,64},{64,96},{96,128},{128,160},{160,192},{192,224},{224... | collective-permute-start | bytes 1572872 | tf_op jit(solution)/shard_map/ppermute | solution.py:12
Sparse Core Ops, SparseCore 0:
  83.1 481.9 all-reduce.1
where the time goes:
time: 575 us; the launch traced here: 574 us
  waiting for transfers between devices  484 us (84%)
  starting transfers between devices  23.9 us (4%)
  local copies, waits for them, and re-layouts  21.8 us (4%)
  other arithmetic  19.7 us (3%)
  between operations  16.3 us (3%)
  matrix products  8.1 us (1%)
    psum x1, waiting for transfers between devices, shards(): summed = lax.psum(probe_acc, ('row', 'col'))  451 us
    ppermute x4, waiting for transfers between devices, shifted(): lax.ppermute(value, axis, [(source, source + steps) for source in range(f...  33 us
    ppermute x4, starting transfers between devices, shifted(): lax.ppermute(value, axis, [(source, source + steps) for source in range(f...  23.9 us
  transfers between devices with their start and end apart: 5, of which 4 were waited for; matrix products, arithmetic and copies ran while one was open for 3% of the time, Pallas kernels for 0%

commit v1 on v0

v1 whole, which is shorter than its diff:
```python
import functools
import math

import jax
import jax.numpy as jnp
import ml_dtypes
import numpy as np
from jax import lax
from jax.experimental import pallas as pl
from jax.experimental.pallas import tpu as pltpu
from jax.sharding import PartitionSpec as P


def shifted(value, axis, steps):
    count = lax.axis_size(axis)
    first, last = (max(0, -steps), min(count, count - steps))
    return lax.ppermute(value, axis, [(source, source + steps) for source in range(first, last)])


def dft_tables(length):
    index = np.arange(length, dtype=np.int32)
    phase = (index[:, None] * index[None, :] % length).astype(np.float32) * np.float32(2.0 * math.pi / length)
    factor = np.float32(1.0 / math.sqrt(length))
    real = (np.cos(phase) * factor).astype(ml_dtypes.bfloat16)
    imag = (-np.sin(phase) * factor).astype(ml_dtypes.bfloat16)
    table_a = np.block([[real, imag], [-imag, real]])
    table_b = np.block([[real, -imag], [imag, real]])
    return table_a, table_b


def patch_kernel(
    scal_ref, own_ref, below_ref, beside_ref, probe_ref, amp_ref, ta_ref, tb_ref,
    keep_ref, send_ref, grad_ref,
    patch_s, far_s, grad_s,
):
    modes = probe_ref.shape[0]
    n = own_ref.shape[1]
    row0, col0, live, parity = scal_ref[0], scal_ref[1], scal_ref[2], scal_ref[3]
    rows = lax.broadcasted_iota(jnp.int32, (n, n), 0)
    cols = lax.broadcasted_iota(jnp.int32, (n, n), 1)
    for k in range(2):
        mixed = jnp.where(cols >= col0, jnp.where(rows >= row0, own_ref[k], below_ref[k]), beside_ref[k])
        mixed = pltpu.roll(mixed, (n - row0) % n, 0)
        patch_s[k] = pltpu.roll(mixed, (n - col0) % n, 1)
    power = jnp.zeros((n, n), jnp.float32)
    for m in range(modes):
        pr = probe_ref[m, 0].astype(jnp.float32)
        pi = probe_ref[m, 1].astype(jnp.float32)
        xr, xi = patch_s[0], patch_s[1]
        er = (pr * xr - pi * xi).astype(jnp.bfloat16)
        ei = (pr * xi + pi * xr).astype(jnp.bfloat16)
        low = jnp.concatenate([er, ei], 0)
        mid = jnp.dot(tb_ref[...], low, preferred_element_type=jnp.float32).astype(jnp.bfloat16)
        mid = jnp.concatenate([mid[:n], mid[n:]], 1)
        far = jnp.dot(mid, ta_ref[...], preferred_element_type=jnp.float32)
        far_s[m] = far
        power = power + (far[:, :n] * far[:, :n] + far[:, n:] * far[:, n:])
    scale = amp_ref[...] / jnp.maximum(jnp.sqrt(power), 0.5)
    for m in range(modes):
        fr = (far_s[m, :, :n] * scale).astype(jnp.bfloat16)
        fi = (far_s[m, :, n:] * scale).astype(jnp.bfloat16)
        low = jnp.concatenate([fr, fi], 0)
        mid = jnp.dot(ta_ref[...], low, preferred_element_type=jnp.float32).astype(jnp.bfloat16)
        mid = jnp.concatenate([mid[:n], mid[n:]], 1)
        far_s[m] = jnp.dot(mid, tb_ref[...], preferred_element_type=jnp.float32)
    live_f = live.astype(jnp.float32)
    part = keep_ref.shape[1] // (2 * modes)
    mean = live_f * scal_ref[4].astype(jnp.float32)
    inverse = 1.0 / scal_ref[5].astype(jnp.float32)
    for a in range(keep_ref.shape[0]):
        for q, out_ref in ((0, keep_ref), (1, send_ref)):
            half = parity if q == 0 else 1 - parity
            here = pl.ds(pl.multiple_of(a * 2 * part + half * part, part), part)
            xr, xi = patch_s[0, here, :], patch_s[1, here, :]
            sr, si = xr * (mean * inverse), xi * (mean * inverse)
            gr = jnp.zeros_like(xr)
            gi = jnp.zeros_like(xr)
            for m in range(modes):
                pr = probe_ref[m, 0, here, :].astype(jnp.float32)
                pi = probe_ref[m, 1, here, :].astype(jnp.float32)
                dr = (pr * xr - pi * xi) - far_s[m, here, :n]
                di = (pr * xi + pi * xr) - far_s[m, here, n:]
                gr = gr + (pr * dr + pi * di)
                gi = gi + (pr * di - pi * dr)
                out_ref[a, 2 * m * part:(2 * m + 1) * part, :] = sr * dr + si * di
                out_ref[a, (2 * m + 1) * part:(2 * m + 2) * part, :] = sr * di - si * dr
            grad_s[0, here, :] = gr * live_f
            grad_s[1, here, :] = gi * live_f
    for k in range(2):
        grad_ref[k] = pltpu.roll(pltpu.roll(grad_s[k], row0, 0), col0, 1)


def shards(specimen, probe_modes, amplitude, offsets, counts):
    tile_rows, tile_cols = specimen.shape[1:]
    modes = probe_modes.shape[0]
    n = probe_modes.shape[2]
    n_row, n_col = lax.axis_size("row"), lax.axis_size("col")
    slots = n_row * n_col * offsets.shape[2]
    row_id, col_id = lax.axis_index("row"), lax.axis_index("col")
    half = n_row // 2
    part = n // n_row

    corner = offsets[0, 0, 0] - jnp.stack([row_id * tile_rows, col_id * tile_cols])
    live = (counts[0, 0] > 0).astype(jnp.int32)
    row0, col0 = corner[0], corner[1]
    left_corner = shifted(corner, "col", 1)
    left_row, left_col = left_corner[0], left_corner[1]

    rows = lax.broadcasted_iota(jnp.int32, (1, n, n), 1)
    cols = lax.broadcasted_iota(jnp.int32, (1, n, n), 2)
    below = shifted(specimen, "row", -1)
    beside = shifted(jnp.where(rows >= left_row, specimen, below), "col", -1)

    table_a, table_b = dft_tables(n)
    parity = row_id % 2
    scalars = jnp.stack([row0, col0, live, parity, jnp.int32(1), jnp.int32(slots)]).astype(jnp.int32)
    vmem = pl.BlockSpec(memory_space=pltpu.VMEM)
    keep, send, grad = pl.pallas_call(
        patch_kernel,
        out_shape=(
            jax.ShapeDtypeStruct((half, 2 * modes * part, n), jnp.float32),
            jax.ShapeDtypeStruct((half, 2 * modes * part, n), jnp.float32),
            jax.ShapeDtypeStruct((2, n, n), jnp.float32),
        ),
        in_specs=[pl.BlockSpec(memory_space=pltpu.SMEM)] + [vmem] * 7,
        out_specs=(vmem, vmem, vmem),
        scratch_shapes=[
            pltpu.VMEM((2, n, n), jnp.float32),
            pltpu.VMEM((modes, n, 2 * n), jnp.float32),
            pltpu.VMEM((2, n, n), jnp.float32),
        ],
        compiler_params=pltpu.CompilerParams(vmem_limit_bytes=40 * 1024 * 1024),
    )(scalars, specimen, below, beside, probe_modes, amplitude[0, 0, 0], jnp.asarray(table_a), jnp.asarray(table_b))

    from_left = shifted(grad, "col", 1)
    mine = jnp.where(cols >= col0, grad, 0.0)
    theirs = jnp.where(cols < left_col, from_left, 0.0)
    down = jnp.where(rows < row0, mine, 0.0) + jnp.where(rows < left_row, theirs, 0.0)
    from_above = shifted(down, "row", 1)
    specimen_grad = (
        jnp.where(rows >= row0, mine, 0.0) + jnp.where(rows >= left_row, theirs, 0.0) + from_above
    )

    other = lax.ppermute(send, "row", [(i, i ^ 1) for i in range(n_row)])
    groups = [[i for i in range(n_row) if i % 2 == k] for k in range(2)]
    summed = lax.all_to_all(keep + other, "row", 0, 0, axis_index_groups=groups, tiled=True).sum(0)
    summed = summed.T.reshape(n_col, n // n_col, 2 * modes * part)
    summed = lax.all_to_all(summed, "col", 0, 0, tiled=True).sum(0)
    probe_grad = summed.T.reshape(modes, 2, part, n // n_col)
    return (specimen_grad, probe_grad)


def solution(mesh):
    in_specs = (
        P(None, "row", "col"),
        P(),
        P("row", "col", None, None, None),
        P("row", "col", None, None),
        P("row", "col"),
    )
    out_specs = (P(None, "row", "col"), P(None, None, "row", "col"))
    return jax.shard_map(shards, mesh=mesh, in_specs=in_specs, out_specs=out_specs, check_vma=False)
```

time: 575 us -> 110 us (0.19)
  the two profiles are of different devices: /device:TPU:1 before, /device:TPU:4 now
where the time goes in v1:
time: 110 us; the launch traced here: 109 us
  waiting for transfers between devices  44.5 us (40%)
  starting transfers between devices  44.2 us (40%)
  other arithmetic  8.17 us (7%)
  local copies, waits for them, and re-layouts  5.85 us (5%)
  Pallas kernels  5.28 us (5%)
  between operations  1.46 us (1%)
    ppermute x5, waiting for transfers between devices, shifted(): lax.ppermute(value, axis, [(source, source + steps) for source in range(f...  26.9 us
    all_to_all x1, starting transfers between devices, shards(): summed = lax.all_to_all(summed, 'col', 0, 0, tiled=True).sum(0)  19.9 us
    ppermute x5, starting transfers between devices, shifted(): lax.ppermute(value, axis, [(source, source + steps) for source in range(f...  16.4 us
    all_to_all x1, waiting for transfers between devices, shards(): summed = lax.all_to_all(summed, 'col', 0, 0, tiled=True).sum(0)  16.2 us
    all_to_all x1, starting transfers between devices, shards(): lax.all_to_all(keep + other, 'row', 0, 0, axis_index_groups=groups, tiled...  6 us
    pallas_call x1, Pallas kernels, shards(): pl.pallas_call(patch_kernel, out_shape=(jax.ShapeDtypeStruct((half, 2 * m...  5.28 us
    unnamed x11, local copies, waits for them, and re-layouts  3.67 us
  transfers between devices with their start and end apart: 8, of which 5 were waited for; matrix products, arithmetic and copies ran while one was open for 8% of the time, Pallas kernels for 0%

profile of v1, /device:TPU:4, one launch (start us, length us, event | category | flops | bytes accessed | tf_op | source)
XLA Modules:
  0.0 109.5 jit_solution(1342449920786884377)
XLA Ops:
  0.6 0.0 copy-start.1
  0.6 2.1 %collective-permute-start = (f32[2,256,256]{2,1,0:T(8,128)}, f32[2,256,256]{2,1,0:T(8,128)S(1)}, u32[]{:S(2)}, u32[]{:S(2)}) collective-permute-start(f32[2,256,256]{2,1,0:T(8,128)} %own_ref.1), channel_id=1, source_target_pairs={{32,0},{64,32},{96,64},{128,96},{160,128},{192,160},{224,192},{256... | collective-permute-start | bytes 1572872 | tf_op jit(solution)/shard_map/ppermute | solution.py:17
  2.7 0.7 add_subtract_fusion
  3.4 5.1 %collective-permute-start.1 = (s32[2]{0:T(128)S(1)}, s32[2]{0:T(128)S(1)}, u32[]{:S(2)}, u32[]{:S(2)}) collective-permute-start(s32[2]{0:T(128)S(1)} %add_subtract_fusion), channel_id=1, source_target_pairs={{0,1},{1,2},{2,3},{3,4},{4,5},{5,6},{6,7},{7,8},{8,9},{9,10},{10,1... | collective-permute-start | bytes 32 | tf_op jit(solution)/shard_map/ppermute | solution.py:17
  8.5 1.3 %collective-permute-done.1 = s32[2]{0:T(128)S(1)} collective-permute-done((s32[2]{0:T(128)S(1)}, s32[2]{0:T(128)S(1)}, u32[]{:S(2)}, u32[]{:S(2)}) %collective-permute-start.1) | collective-permute-done | bytes 40 | tf_op jit(solution)/shard_map/ppermute | solution.py:17
  9.8 0.7 fusion.1
  10.5 0.6 iota_compare_fusion.3
  11.1 0.0 copy-start
  11.1 0.0 collective-permute-done.below_ref
  11.1 1.2 %broadcast_select_fusion = f32[2,256,256]{2,1,0:T(8,128)S(1)} fusion(f32[2,256,256]{2,1,0:T(8,128)} %own_ref.1, f32[2,256,256]{2,1,0:T(8,128)S(1)} %collective-permute-done.below_ref, pred[256]{0:T(512)(128)(4,1)S(1)} %iota_compare_fusion.3), kind=kLoop, calls=%fused_computation.2 | loop fusion | flops 131072 | bytes 1573120 | tf_op jit(solution)/shard_map/jit(_where)/select_n | solution.py:112
  12.4 1.3 %collective-permute-start.2 = (f32[2,256,256]{2,1,0:T(8,128)S(1)}, f32[2,256,256]{2,1,0:T(8,128)S(1)}, u32[]{:S(2)}, u32[]{:S(2)}) collective-permute-start(f32[2,256,256]{2,1,0:T(8,128)S(1)} %broadcast_select_fusion), channel_id=1, source_target_pairs={{1,0},{2,1},{3,2},{4,3},{5,4},{6,5},{7,6},{8,7},{9,8},{10,9},{11,1... | collective-permute-start | bytes 1572872 | tf_op jit(solution)/shard_map/ppermute | solution.py:17
  14.3 0.1 stack.27.scal_ref
  14.4 15.3 %collective-permute-done.2.beside_ref = f32[2,256,256]{2,1,0:T(8,128)S(1)} collective-permute-done((f32[2,256,256]{2,1,0:T(8,128)S(1)}, f32[2,256,256]{2,1,0:T(8,128)S(1)}, u32[]{:S(2)}, u32[]{:S(2)}) %collective-permute-start.2) | collective-permute-done | bytes 524320 | tf_op jit(solution)/shard_map/ppermute | solution.py:17
  29.7 0.0 copy-done.1
  29.7 0.0 copy-done
  29.7 0.0 copy-start.2
  29.7 1.0 copy-done.2
  30.8 0.0 copy-start.3
  30.8 1.0 copy-done.3
  31.8 0.0 copy-start.4
  31.8 0.9 copy-done.4
  32.7 5.3 %shard_map.86 = (f32[8,128,256]{2,1,0:T(8,128)S(1)}, f32[8,128,256]{2,1,0:T(8,128)S(1)}, f32[2,256,256]{2,1,0:T(8,128)S(1)}) custom-call(s32[6]{0:T(128)S(1)} %stack.27.scal_ref, f32[2,256,256]{2,1,0:T(8,128)S(1)} %copy-done, f32[2,256,256]{2,1,0:T(8,128)S(1)} %collective-permute-done.below_ref, f32[2,256,256]{2,1,0:T(8,128)S(1)} %collective-permute-done.2.beside_ref, ...), custom_call_target="tpu_custom_call" | custom-call | tf_op jit(solution)/shard_map/pallas_call | solution.py:118
  38.0 1.9 %collective-permute-start.5 = (f32[8,128,256]{2,1,0:T(8,128)S(1)}, f32[8,128,256]{2,1,0:T(8,128)S(1)}, u32[]{:S(2)}, u32[]{:S(2)}) collective-permute-start(f32[8,128,256]{2,1,0:T(8,128)S(1)} %get-tuple-element.7), channel_id=1, source_target_pairs={{0,32},{32,0},{64,96},{96,64},{128,160},{160,128},{192,224},{224,1... | collective-permute-start | bytes 3145736 | tf_op jit(solution)/shard_map/ppermute | solution.py:144
  40.0 6.0 %collective-permute-start.3 = (f32[2,256,256]{2,1,0:T(8,128)S(1)}, f32[2,256,256]{2,1,0:T(8,128)S(1)}, u32[]{:S(2)}, u32[]{:S(2)}) collective-permute-start(f32[2,256,256]{2,1,0:T(8,128)S(1)} %get-tuple-element.5), channel_id=1, source_target_pairs={{0,1},{1,2},{2,3},{3,4},{4,5},{5,6},{6,7},{7,8},{8,9},{9,10},{10,1... | collective-permute-start | bytes 1572872 | tf_op jit(solution)/shard_map/ppermute | solution.py:17
  46.0 0.0 collective-permute-done.5
  46.0 1.1 %add.20 = f32[8,128,256]{2,1,0:T(8,128)} add(f32[8,128,256]{2,1,0:T(8,128)S(1)} %get-tuple-element.6, f32[8,128,256]{2,1,0:T(8,128)S(1)} %collective-permute-done.5) | non-fusion elementwise | flops 262144 | bytes 3145728 | tf_op jit(solution)/shard_map/add | solution.py:146
  47.1 6.0 %all-to-all-start = ((f32[8,128,256]{2,1,0:T(8,128)}), f32[8,128,256]{2,1,0:T(8,128)S(1)}, u32[]{:S(2)}, u32[]{:S(2)}) async-start(f32[8,128,256]{2,1,0:T(8,128)} %add.20), calls=%async_computation | async-start | bytes 2097152 | tf_op jit(solution)/shard_map/all_to_all | solution.py:146
  53.1 0.6 fusion
  53.7 1.3 %iota_compare_fusion = (pred[256]{0:T(512)(128)(4,1)S(1)}, pred[256]{0:T(512)(128)(4,1)S(1)}) fusion(s32[]{:T(128)} %bitcast.7, s32[]{:T(128)} %bitcast.3), kind=kLoop, calls=%fused_computation.3 | loop fusion | flops 512 | bytes 520 | tf_op jit(solution)/shard_map/lt | solution.py:138
  55.0 1.3 %iota_compare_fusion.2 = (pred[256]{0:T(512)(128)(4,1)S(1)}, pred[256]{0:T(512)(128)(4,1)S(1)}) fusion(s32[]{:T(128)} %bitcast.9, s32[]{:T(128)} %bitcast.4), kind=kLoop, calls=%fused_computation.5 | loop fusion | flops 512 | bytes 520 | tf_op jit(solution)/shard_map/lt | solution.py:137
  56.3 10.3 %collective-permute-done.3 = f32[2,256,256]{2,1,0:T(8,128)S(1)} collective-permute-done((f32[2,256,256]{2,1,0:T(8,128)S(1)}, f32[2,256,256]{2,1,0:T(8,128)S(1)}, u32[]{:S(2)}, u32[]{:S(2)}) %collective-permute-start.3) | collective-permute-done | bytes 524320 | tf_op jit(solution)/shard_map/ppermute | solution.py:17
  66.6 0.2 select_add_fusion
  66.8 1.9 %collective-permute-start.4 = (f32[2,256,256]{2,1,0:T(8,128)S(1)}, f32[2,256,256]{2,1,0:T(8,128)S(1)}, u32[]{:S(2)}, u32[]{:S(2)}) collective-permute-start(f32[2,256,256]{2,1,0:T(8,128)S(1)} %select_add_fusion), channel_id=1, source_target_pairs={{0,32},{32,64},{64,96},{96,128},{128,160},{160,192},{192,224},{224... | collective-permute-start | bytes 1572872 | tf_op jit(solution)/shard_map/ppermute | solution.py:17
  68.7 1.5 %all-to-all-done = f32[8,128,256]{2,1,0:T(8,128)S(1)} async-done(((f32[8,128,256]{2,1,0:T(8,128)}), f32[8,128,256]{2,1,0:T(8,128)S(1)}, u32[]{:S(2)}, u32[]{:S(2)}) %all-to-all-start) | async-done | bytes 1048608 | tf_op jit(solution)/shard_map/all_to_all | solution.py:146
  70.2 0.1 reduce_sum.18
  70.2 0.8 copy.10
  71.0 19.9 %all-to-all-start.1 = ((f32[32,8,128]{2,1,0:T(8,128)}), f32[32,8,128]{2,1,0:T(8,128)S(1)}, u32[]{:S(2)}, u32[]{:S(2)}) async-start(f32[32,8,128]{2,1,0:T(8,128)} %bitcast.11), calls=%async_computation.1 | async-start | bytes 262144 | tf_op jit(solution)/shard_map/all_to_all | solution.py:148
  90.9 0.7 iota_compare_fusion.5
  91.5 0.0 collective-permute-done.4
  91.5 1.0 add_add_fusion
  92.5 16.2 %all-to-all-done.1 = f32[32,8,128]{2,1,0:T(8,128)S(1)} async-done(((f32[32,8,128]{2,1,0:T(8,128)}), f32[32,8,128]{2,1,0:T(8,128)S(1)}, u32[]{:S(2)}, u32[]{:S(2)}) %all-to-all-start.1) | async-done | bytes 131104 | tf_op jit(solution)/shard_map/all_to_all | solution.py:148
  108.7 0.1 reshape.15
  108.9 0.6 copy.11
  (1 shorter events, 0.0 us)
Async XLA Ops:
  0.6 29.1 %copy-start.1 = (bf16[4,2,256,256]{3,2,1,0:T(8,128)(2,1)S(1)}, bf16[4,2,256,256]{3,2,1,0:T(8,128)(2,1)}, u32[]{:S(2)}) copy-start(bf16[4,2,256,256]{3,2,1,0:T(8,128)(2,1)} %probe_ref.1) | copy-start | bytes 3145732
  0.6 10.5 %collective-permute-start = (f32[2,256,256]{2,1,0:T(8,128)}, f32[2,256,256]{2,1,0:T(8,128)S(1)}, u32[]{:S(2)}, u32[]{:S(2)}) collective-permute-start(f32[2,256,256]{2,1,0:T(8,128)} %own_ref.1), channel_id=1, source_target_pairs={{32,0},{64,32},{96,64},{128,96},{160,128},{192,160},{224,192},{256... | collective-permute-start | bytes 1572872 | tf_op jit(solution)/shard_map/ppermute | solution.py:17
  3.4 6.4 %collective-permute-start.1 = (s32[2]{0:T(128)S(1)}, s32[2]{0:T(128)S(1)}, u32[]{:S(2)}, u32[]{:S(2)}) collective-permute-start(s32[2]{0:T(128)S(1)} %add_subtract_fusion), channel_id=1, source_target_pairs={{0,1},{1,2},{2,3},{3,4},{4,5},{5,6},{6,7},{7,8},{8,9},{9,10},{10,1... | collective-permute-start | bytes 32 | tf_op jit(solution)/shard_map/ppermute | solution.py:17
  11.1 18.6 %copy-start = (f32[2,256,256]{2,1,0:T(8,128)S(1)}, f32[2,256,256]{2,1,0:T(8,128)}, u32[]{:S(2)}) copy-start(f32[2,256,256]{2,1,0:T(8,128)} %own_ref.1) | copy-start | bytes 1572868
  12.4 17.4 %collective-permute-start.2 = (f32[2,256,256]{2,1,0:T(8,128)S(1)}, f32[2,256,256]{2,1,0:T(8,128)S(1)}, u32[]{:S(2)}, u32[]{:S(2)}) collective-permute-start(f32[2,256,256]{2,1,0:T(8,128)S(1)} %broadcast_select_fusion), channel_id=1, source_target_pairs={{1,0},{2,1},{3,2},{4,3},{5,4},{6,5},{7,6},{8,7},{9,8},{10,9},{11,1... | collective-permute-start | bytes 1572872 | tf_op jit(solution)/shard_map/ppermute | solution.py:17
  29.7 1.0 copy-start.2
  30.8 1.0 copy-start.3
  31.8 0.9 copy-start.4
  38.0 8.0 %collective-permute-start.5 = (f32[8,128,256]{2,1,0:T(8,128)S(1)}, f32[8,128,256]{2,1,0:T(8,128)S(1)}, u32[]{:S(2)}, u32[]{:S(2)}) collective-permute-start(f32[8,128,256]{2,1,0:T(8,128)S(1)} %get-tuple-element.7), channel_id=1, source_target_pairs={{0,32},{32,0},{64,96},{96,64},{128,160},{160,128},{192,224},{224,1... | collective-permute-start | bytes 3145736 | tf_op jit(solution)/shard_map/ppermute | solution.py:144
  40.0 26.7 %collective-permute-start.3 = (f32[2,256,256]{2,1,0:T(8,128)S(1)}, f32[2,256,256]{2,1,0:T(8,128)S(1)}, u32[]{:S(2)}, u32[]{:S(2)}) collective-permute-start(f32[2,256,256]{2,1,0:T(8,128)S(1)} %get-tuple-element.5), channel_id=1, source_target_pairs={{0,1},{1,2},{2,3},{3,4},{4,5},{5,6},{6,7},{7,8},{8,9},{9,10},{10,1... | collective-permute-start | bytes 1572872 | tf_op jit(solution)/shard_map/ppermute | solution.py:17
  47.1 23.0 %all-to-all-start = ((f32[8,128,256]{2,1,0:T(8,128)}), f32[8,128,256]{2,1,0:T(8,128)S(1)}, u32[]{:S(2)}, u32[]{:S(2)}) async-start(f32[8,128,256]{2,1,0:T(8,128)} %add.20), calls=%async_computation | async-start | bytes 2097152 | tf_op jit(solution)/shard_map/all_to_all | solution.py:146
  66.8 24.8 %collective-permute-start.4 = (f32[2,256,256]{2,1,0:T(8,128)S(1)}, f32[2,256,256]{2,1,0:T(8,128)S(1)}, u32[]{:S(2)}, u32[]{:S(2)}) collective-permute-start(f32[2,256,256]{2,1,0:T(8,128)S(1)} %select_add_fusion), channel_id=1, source_target_pairs={{0,32},{32,64},{64,96},{96,128},{128,160},{160,192},{192,224},{224... | collective-permute-start | bytes 1572872 | tf_op jit(solution)/shard_map/ppermute | solution.py:17
  71.0 37.7 %all-to-all-start.1 = ((f32[32,8,128]{2,1,0:T(8,128)}), f32[32,8,128]{2,1,0:T(8,128)S(1)}, u32[]{:S(2)}, u32[]{:S(2)}) async-start(f32[32,8,128]{2,1,0:T(8,128)} %bitcast.11), calls=%async_computation.1 | async-start | bytes 262144 | tf_op jit(solution)/shard_map/all_to_all | solution.py:148

commit v2 on v1

v2 whole, which is shorter than its diff:
```python
import functools
import math

import jax
import jax.numpy as jnp
import ml_dtypes
import numpy as np
from jax import lax
from jax.experimental import pallas as pl
from jax.experimental.pallas import tpu as pltpu
from jax.sharding import Mesh
from jax.sharding import PartitionSpec as P

ROW = ("ylo", "x", "core")
COL = ("z", "yhi")
FIRST_ROWS = 144


def shifted(value, axis, steps):
    count = lax.axis_size(axis)
    first, last = (max(0, -steps), min(count, count - steps))
    return lax.ppermute(value, axis, [(source, source + steps) for source in range(first, last)])


def dft_tables(length):
    index = np.arange(length, dtype=np.int32)
    phase = (index[:, None] * index[None, :] % length).astype(np.float32) * np.float32(2.0 * math.pi / length)
    factor = np.float32(1.0 / math.sqrt(length))
    real = (np.cos(phase) * factor).astype(ml_dtypes.bfloat16)
    imag = (-np.sin(phase) * factor).astype(ml_dtypes.bfloat16)
    return np.block([[real, imag], [-imag, real]]), np.block([[real, -imag], [imag, real]])


def mix_kernel(corner_ref, own_ref, right_ref, out_ref):
    cols = lax.broadcasted_iota(jnp.int32, own_ref.shape, 2)
    out_ref[...] = jnp.where(cols >= corner_ref[1], own_ref[...], right_ref[...])


def side_kernel(scal_ref, own0_ref, own1_ref, right0_ref, right1_ref, probe_in, amp_in, ta_in, tb_in,
                side_ref, probe_ref, amp_ref, ta_ref, tb_ref):
    first = own0_ref.shape[1]
    cols = lax.broadcasted_iota(jnp.int32, side_ref.shape, 2)
    side_ref[:, :first] = jnp.where(cols[:, :first] >= scal_ref[1], own0_ref[...], right0_ref[...])
    side_ref[:, first:] = jnp.where(cols[:, first:] >= scal_ref[1], own1_ref[...], right1_ref[...])
    for src, dst in ((probe_in, probe_ref), (amp_in, amp_ref), (ta_in, ta_ref), (tb_in, tb_ref)):
        dst[...] = src[...]


def split_kernel(scal_ref, grad_ref, left_ref, mine_ref, down_ref):
    n = mine_ref.shape[1]
    row0, col0 = scal_ref[0], scal_ref[1]
    rows = lax.broadcasted_iota(jnp.int32, (n, n), 0)
    cols = lax.broadcasted_iota(jnp.int32, (n, n), 1)
    left_rows = rows.astype(jnp.float32) >= left_ref[0, n:n + 1]
    left_cols = cols.astype(jnp.float32) < left_ref[1, n:n + 1]
    for k in range(2):
        own = jnp.where(cols >= col0, grad_ref[k, :n], 0.0)
        left = jnp.where(left_cols, left_ref[k, :n], 0.0)
        mine_ref[k] = jnp.where(rows >= row0, own, 0.0) + jnp.where(left_rows, left, 0.0)
        down_ref[k] = jnp.where(rows < row0, own, 0.0) + jnp.where(left_rows, 0.0, left)


def pair_kernel(keep_ref, other_ref, out_ref):
    count, wide, n = keep_ref.shape
    n_x, _, n_y, n_z, eight = out_ref.shape[:5]
    for a in range(count):
        turned = (keep_ref[a] + other_ref[a]).T.reshape(n_z, 2, eight, wide)
        out_ref[a % n_x, 0, a // n_x] = turned[:, 0]
        out_ref[a % n_x, 1, a // n_x] = turned[:, 1]


def patch_kernel(
    inverse_slots, scal_ref, side_ref, under0_ref, under1_ref, probe_ref, amp_ref, ta_ref, tb_ref,
    keep_ref, send_ref, grad_ref,
    patch_s, far_s, grad_s, mid_s,
):
    modes = probe_ref.shape[0]
    n = side_ref.shape[1]
    row0, col0, live, parity = scal_ref[0], scal_ref[1], scal_ref[2], scal_ref[3]
    rows = lax.broadcasted_iota(jnp.int32, (n, n), 0)
    for k in range(2):
        under = jnp.concatenate([under0_ref[k], under1_ref[k]], 0)
        mixed = jnp.where(rows >= row0, side_ref[k], under)
        mixed = pltpu.roll(mixed, (n - row0) % n, 0)
        patch_s[k] = pltpu.roll(mixed, (n - col0) % n, 1)
    xr, xi = patch_s[0], patch_s[1]
    for m in range(modes):
        pr = probe_ref[m, 0].astype(jnp.float32)
        pi = probe_ref[m, 1].astype(jnp.float32)
        er = (pr * xr - pi * xi).astype(jnp.bfloat16)
        ei = (pr * xi + pi * xr).astype(jnp.bfloat16)
        mid = jnp.dot(tb_ref[...], jnp.concatenate([er, ei], 0), preferred_element_type=jnp.float32)
        mid_s[m * n:(m + 1) * n, :n] = mid[:n].astype(jnp.bfloat16)
        mid_s[m * n:(m + 1) * n, n:] = mid[n:].astype(jnp.bfloat16)
    far_s[...] = jnp.dot(mid_s[...], ta_ref[...], preferred_element_type=jnp.float32).reshape(modes, n, 2 * n)
    power = jnp.zeros((n, n), jnp.float32)
    for m in range(modes):
        power = power + (far_s[m, :, :n] * far_s[m, :, :n] + far_s[m, :, n:] * far_s[m, :, n:])
    scale = amp_ref[...] / jnp.maximum(jnp.sqrt(power), 0.5)
    for m in range(modes):
        fr = (far_s[m, :, :n] * scale).astype(jnp.bfloat16)
        fi = (far_s[m, :, n:] * scale).astype(jnp.bfloat16)
        mid = jnp.dot(ta_ref[...], jnp.concatenate([fr, fi], 0), preferred_element_type=jnp.float32)
        mid_s[m * n:(m + 1) * n, :n] = mid[:n].astype(jnp.bfloat16)
        mid_s[m * n:(m + 1) * n, n:] = mid[n:].astype(jnp.bfloat16)
    far_s[...] = jnp.dot(mid_s[...], tb_ref[...], preferred_element_type=jnp.float32).reshape(modes, n, 2 * n)
    live_f = live.astype(jnp.float32)
    part = keep_ref.shape[1] // (2 * modes)
    mean = live_f * inverse_slots
    for a in range(keep_ref.shape[0]):
        for q, out_ref in ((0, keep_ref), (1, send_ref)):
            half = parity if q == 0 else 1 - parity
            here = pl.ds(pl.multiple_of(a * 2 * part + half * part, part), part)
            xr, xi = patch_s[0, here, :], patch_s[1, here, :]
            sr, si = xr * mean, xi * mean
            gr = jnp.zeros_like(xr)
            gi = jnp.zeros_like(xr)
            for m in range(modes):
                pr = probe_ref[m, 0, here, :].astype(jnp.float32)
                pi = probe_ref[m, 1, here, :].astype(jnp.float32)
                dr = (pr * xr - pi * xi) - far_s[m, here, :n]
                di = (pr * xi + pi * xr) - far_s[m, here, n:]
                gr = gr + (pr * dr + pi * di)
                gi = gi + (pr * di - pi * dr)
                out_ref[a, 2 * m * part:(2 * m + 1) * part, :] = sr * dr + si * di
                out_ref[a, (2 * m + 1) * part:(2 * m + 2) * part, :] = sr * di - si * dr
            grad_s[0, here, :] = gr * live_f
            grad_s[1, here, :] = gi * live_f
    for k in range(2):
        grad_ref[k, :n] = pltpu.roll(pltpu.roll(grad_s[k], row0, 0), col0, 1)
        grad_ref[k, n:] = jnp.full((grad_ref.shape[1] - n, n), scal_ref[k], jnp.int32).astype(jnp.float32)


def shards(specimen, probe_modes, amplitude, offsets, counts):
    tile_rows, tile_cols = specimen.shape[1:]
    modes = probe_modes.shape[0]
    n = probe_modes.shape[2]
    n_row, n_col = lax.axis_size(ROW), lax.axis_size(COL)
    slots = n_row * n_col * offsets.shape[2]
    row_id, col_id = lax.axis_index(ROW), lax.axis_index(COL)
    n_x, half = lax.axis_size("x"), n_row // 2
    part = n // n_row

    corner = offsets[0, 0, 0] - jnp.stack([row_id * tile_rows, col_id * tile_cols])
    live = (counts[0, 0] > 0).astype(jnp.int32)
    row0, col0 = corner[0], corner[1]

    own = [specimen[:, :FIRST_ROWS], lax.optimization_barrier(specimen)[:, FIRST_ROWS:]]
    right = [shifted(part_rows, COL, -1) for part_rows in own]
    vmem = pl.BlockSpec(memory_space=pltpu.VMEM)
    smem = pl.BlockSpec(memory_space=pltpu.SMEM)
    above_corner = shifted(corner, ROW, 1)
    mixed = [
        pl.pallas_call(
            mix_kernel,
            out_shape=jax.ShapeDtypeStruct(mine.shape, jnp.float32),
            in_specs=[smem, vmem, vmem],
            out_specs=vmem,
            compiler_params=pltpu.CompilerParams(vmem_limit_bytes=2 << 20),
        )(above_corner, mine, beside)
        for mine, beside in zip(own, right)
    ]
    under = [shifted(part_rows, ROW, -1) for part_rows in mixed]

    scalars = jnp.stack([row0, col0, live, row_id % 2]).astype(jnp.int32)
    table_a, table_b = dft_tables(n)
    operands = (probe_modes, amplitude[0, 0, 0], jnp.asarray(table_a), jnp.asarray(table_b))
    side, *operands = pl.pallas_call(
        side_kernel,
        out_shape=(jax.ShapeDtypeStruct((2, n, n), jnp.float32),)
        + tuple(jax.ShapeDtypeStruct(value.shape, value.dtype) for value in operands),
        in_specs=[smem] + [vmem] * 8,
        out_specs=(vmem,) * 5,
        compiler_params=pltpu.CompilerParams(vmem_limit_bytes=10 << 20),
    )(scalars, *own, *right, *operands)
    keep, send, grad = pl.pallas_call(
        functools.partial(patch_kernel, 1.0 / slots),
        out_shape=(
            jax.ShapeDtypeStruct((half, 2 * modes * part, n), jnp.float32),
            jax.ShapeDtypeStruct((half, 2 * modes * part, n), jnp.float32),
            jax.ShapeDtypeStruct((2, n + 8, n), jnp.float32),
        ),
        in_specs=[smem] + [vmem] * 7,
        out_specs=(vmem,) * 3,
        scratch_shapes=[
            pltpu.VMEM((2, n, n), jnp.float32),
            pltpu.VMEM((modes, n, 2 * n), jnp.float32),
            pltpu.VMEM((2, n, n), jnp.float32),
            pltpu.VMEM((modes * n, 2 * n), jnp.bfloat16),
        ],
        compiler_params=pltpu.CompilerParams(vmem_limit_bytes=14 << 20),
    )(scalars, side, *under, *operands)

    other = lax.ppermute(send, "core", [(0, 1), (1, 0)])
    from_left = shifted(grad, COL, 1)
    summed = pl.pallas_call(
        pair_kernel,
        out_shape=jax.ShapeDtypeStruct((n_x, 2, half // n_x, n_col // 2, n // n_col, 2 * modes * part), jnp.float32),
        in_specs=[vmem] * 2,
        out_specs=vmem,
        compiler_params=pltpu.CompilerParams(vmem_limit_bytes=8 << 20),
    )(keep, other)
    summed = lax.all_to_all(summed, "x", 0, 0, tiled=True)
    mine, down = pl.pallas_call(
        split_kernel,
        out_shape=(jax.ShapeDtypeStruct((2, n, n), jnp.float32),) * 2,
        in_specs=[smem, vmem, vmem],
        out_specs=(vmem,) * 2,
        compiler_params=pltpu.CompilerParams(vmem_limit_bytes=4 << 20),
    )(scalars, grad, from_left)
    from_above = shifted(down, ROW, 1)
    summed = summed.sum(0).reshape((2 * n_col,) + summed.shape[-2:])
    summed = lax.all_to_all(summed, ("yhi", "ylo", "z"), 0, 0, tiled=True).sum(0)
    probe_grad = summed.T.reshape(modes, 2, part, n // n_col)
    specimen_grad = mine + from_above
    return (specimen_grad, probe_grad)


def solution(mesh):
    n_row, n_col = mesh.devices.shape
    fine = Mesh(mesh.devices.reshape(2, n_row // 4, 2, n_col // 2, 2), ROW + COL)
    in_specs = (
        P(None, ROW, COL),
        P(),
        P(ROW, COL, None, None, None),
        P(ROW, COL, None, None),
        P(ROW, COL),
    )
    out_specs = (P(None, ROW, COL), P(None, None, ROW, COL))
    return jax.shard_map(shards, mesh=fine, in_specs=in_specs, out_specs=out_specs, check_vma=False)
```

time: 110 us -> 102 us (0.927)
  the two profiles are of different devices: /device:TPU:4 before, /device:TPU:8 now
where the time goes in v2:
time: 102 us; the launch traced here: 101 us
  starting transfers between devices  44.5 us (44%)
  waiting for transfers between devices  39.8 us (39%)
  Pallas kernels  10.1 us (10%)
  local copies, waits for them, and re-layouts  3.64 us (4%)
  other arithmetic  1.85 us (2%)
  between operations  1.48 us (1%)
    ppermute x7, waiting for transfers between devices, shifted(): lax.ppermute(value, axis, [(source, source + steps) for source in range(f...  22.3 us
    all_to_all x1, starting transfers between devices, shards(): lax.all_to_all(summed, ('yhi', 'ylo', 'z'), 0, 0, tiled=True).sum(0)  21.3 us
    ppermute x7, starting transfers between devices, shifted(): lax.ppermute(value, axis, [(source, source + steps) for source in range(f...  17.4 us
    all_to_all x1, waiting for transfers between devices, shards(): summed = lax.all_to_all(summed, 'x', 0, 0, tiled=True)  10.4 us
    pallas_call x1, Pallas kernels, shards(): pl.pallas_call(functools.partial(patch_kernel, 1.0 / slots), out_shape=(j...  5.45 us
    all_to_all x1, waiting for transfers between devices, shards(): lax.all_to_all(summed, ('yhi', 'ylo', 'z'), 0, 0, tiled=True).sum(0)  4.58 us
    all_to_all x1, starting transfers between devices, shards(): summed = lax.all_to_all(summed, 'x', 0, 0, tiled=True)  3.78 us
    ppermute x1, waiting for transfers between devices, shards(): other = lax.ppermute(send, 'core', [(0, 1), (1, 0)])  2.5 us
  transfers between devices with their start and end apart: 10, of which 8 were waited for; matrix products, arithmetic and copies ran while one was open for 3% of the time, Pallas kernels for 3%

profile of v2, /device:TPU:8, one launch (start us, length us, event | category | flops | bytes accessed | tf_op | source)
XLA Modules:
  0.0 101.4 jit_solution(14729936890605994776)
XLA Ops:
  0.6 0.0 copy-start.4
  0.6 1.0 slice.9.own0_ref.own_ref
  1.6 0.0 copy-start
  1.6 1.4 %collective-permute-start = (f32[2,144,256]{2,1,0:T(8,128)S(1)}, f32[2,144,256]{2,1,0:T(8,128)S(1)}, u32[]{:S(2)}, u32[]{:S(2)}) collective-permute-start(f32[2,144,256]{2,1,0:T(8,128)S(1)} %slice.9.own0_ref.own_ref), channel_id=1, source_target_pairs={{1,0},{2,1},{3,2},{4,3},{5,4},{6,5},{7,6},{8,7},{9,8},{10,9},{11,1... | collective-permute-start | bytes 884744 | tf_op jit(solution)/shard_map/ppermute | solution.py:22
  3.1 1.0 slice.11.own1_ref.own_ref
  4.0 1.3 %collective-permute-start.1 = (f32[2,112,256]{2,1,0:T(8,128)S(1)}, f32[2,112,256]{2,1,0:T(8,128)S(1)}, u32[]{:S(2)}, u32[]{:S(2)}) collective-permute-start(f32[2,112,256]{2,1,0:T(8,128)S(1)} %slice.11.own1_ref.own_ref), channel_id=1, source_target_pairs={{1,0},{2,1},{3,2},{4,3},{5,4},{6,5},{7,6},{8,7},{9,8},{10,9},{11,1... | collective-permute-start | bytes 688136 | tf_op jit(solution)/shard_map/ppermute | solution.py:22
  5.4 0.0 copy-done.4
  5.4 0.1 add_subtract_fusion
  5.4 1.9 %collective-permute-start.2 = (s32[2]{0:T(128)S(1)}, s32[2]{0:T(128)S(1)}, u32[]{:S(2)}, u32[]{:S(2)}) collective-permute-start(s32[2]{0:T(128)S(1)} %add_subtract_fusion), channel_id=1, source_target_pairs={{0,32},{32,64},{64,96},{96,128},{128,160},{160,192},{192,224},{224... | collective-permute-start | bytes 32 | tf_op jit(solution)/shard_map/ppermute | solution.py:22
  7.4 5.0 %collective-permute-done.2.corner_ref = s32[2]{0:T(128)S(1)} collective-permute-done((s32[2]{0:T(128)S(1)}, s32[2]{0:T(128)S(1)}, u32[]{:S(2)}, u32[]{:S(2)}) %collective-permute-start.2) | collective-permute-done | bytes 40 | tf_op jit(solution)/shard_map/ppermute | solution.py:22
  12.4 2.7 %collective-permute-done.right0_ref.right_ref = f32[2,144,256]{2,1,0:T(8,128)S(1)} collective-permute-done((f32[2,144,256]{2,1,0:T(8,128)S(1)}, f32[2,144,256]{2,1,0:T(8,128)S(1)}, u32[]{:S(2)}, u32[]{:S(2)}) %collective-permute-start) | collective-permute-done | bytes 294944 | tf_op jit(solution)/shard_map/ppermute | solution.py:22
  15.1 0.0 copy-start.2
  15.1 0.6 shard_map.87
  15.6 0.0 copy-start.1
  15.7 2.1 %collective-permute-start.3 = (f32[2,144,256]{2,1,0:T(8,128)S(1)}, f32[2,144,256]{2,1,0:T(8,128)}, u32[]{:S(2)}, u32[]{:S(2)}) collective-permute-start(f32[2,144,256]{2,1,0:T(8,128)S(1)} %shard_map.87), channel_id=1, source_target_pairs={{32,0},{64,32},{96,64},{128,96},{160,128},{192,160},{224,192},{256... | collective-permute-start | bytes 884744 | tf_op jit(solution)/shard_map/ppermute | solution.py:22
  17.8 1.1 %collective-permute-done.1.right1_ref.right_ref = f32[2,112,256]{2,1,0:T(8,128)S(1)} collective-permute-done((f32[2,112,256]{2,1,0:T(8,128)S(1)}, f32[2,112,256]{2,1,0:T(8,128)S(1)}, u32[]{:S(2)}, u32[]{:S(2)}) %collective-permute-start.1) | collective-permute-done | bytes 229408 | tf_op jit(solution)/shard_map/ppermute | solution.py:22
  18.8 1.3 %shard_map.88 = f32[2,112,256]{2,1,0:T(8,128)} custom-call(s32[2]{0:T(128)S(1)} %collective-permute-done.2.corner_ref, f32[2,112,256]{2,1,0:T(8,128)S(1)} %slice.11.own1_ref.own_ref, f32[2,112,256]{2,1,0:T(8,128)S(1)} %collective-permute-done.1.right1_ref.right_ref), custom_call_target="tpu_custom_call" | custom-call | tf_op jit(solution)/shard_map/pallas_call | solution.py:154
  20.1 3.5 %collective-permute-start.4 = (f32[2,112,256]{2,1,0:T(8,128)}, f32[2,112,256]{2,1,0:T(8,128)}, u32[]{:S(2)}, u32[]{:S(2)}) collective-permute-start(f32[2,112,256]{2,1,0:T(8,128)} %shard_map.88), channel_id=1, source_target_pairs={{32,0},{64,32},{96,64},{128,96},{160,128},{192,160},{224,192},{256... | collective-permute-start | bytes 688136 | tf_op jit(solution)/shard_map/ppermute | solution.py:22
  24.3 0.1 pad_add_fusion.scal_ref
  24.4 0.0 copy-done
  24.4 0.0 copy-done.2
  24.4 0.0 copy-done.1
  24.4 0.0 copy-start.3
  24.4 0.9 copy-done.3
  25.3 0.7 shard_map.86
  26.1 1.4 %collective-permute-done.4.under1_ref = f32[2,112,256]{2,1,0:T(8,128)} collective-permute-done((f32[2,112,256]{2,1,0:T(8,128)}, f32[2,112,256]{2,1,0:T(8,128)}, u32[]{:S(2)}, u32[]{:S(2)}) %collective-permute-start.4) | collective-permute-done | bytes 229408 | tf_op jit(solution)/shard_map/ppermute | solution.py:22
  27.5 0.0 collective-permute-done.3.under0_ref
  27.5 5.5 %shard_map.89 = (f32[8,128,256]{2,1,0:T(8,128)S(1)}, f32[8,128,256]{2,1,0:T(8,128)S(1)}, f32[2,264,256]{2,1,0:T(8,128)S(1)}) custom-call(s32[4]{0:T(128)S(1)} %pad_add_fusion.scal_ref, f32[2,256,256]{2,1,0:T(8,128)S(1)} %get-tuple-element.12.side_ref, f32[2,144,256]{2,1,0:T(8,128)} %collective-permute-done.3.under0_ref, ...), custom_call_target="tpu_custom_call" | custom-call | tf_op jit(solution)/shard_map/pallas_call | solution.py:176
  32.9 2.0 %collective-permute-start.7 = (f32[8,128,256]{2,1,0:T(8,128)S(1)}, f32[8,128,256]{2,1,0:T(8,128)S(1)}, u32[]{:S(2)}, u32[]{:S(2)}) collective-permute-start(f32[8,128,256]{2,1,0:T(8,128)S(1)} %get-tuple-element.21), channel_id=1, source_target_pairs={{0,32},{32,0},{1,33},{33,1},{2,34},{34,2},{3,35},{35,3},{4,36},{36... | collective-permute-start | bytes 3145736 | tf_op jit(solution)/shard_map/ppermute | solution.py:194
  35.0 2.5 %collective-permute-done.7.other_ref = f32[8,128,256]{2,1,0:T(8,128)S(1)} collective-permute-done((f32[8,128,256]{2,1,0:T(8,128)S(1)}, f32[8,128,256]{2,1,0:T(8,128)S(1)}, u32[]{:S(2)}, u32[]{:S(2)}) %collective-permute-start.7) | collective-permute-done | bytes 1048608 | tf_op jit(solution)/shard_map/ppermute | solution.py:194
  37.5 1.3 %shard_map.91 = f32[4,2,2,16,8,128]{5,4,3,2,1,0:T(8,128)} custom-call(f32[8,128,256]{2,1,0:T(8,128)S(1)} %get-tuple-element.20.keep_ref, f32[8,128,256]{2,1,0:T(8,128)S(1)} %collective-permute-done.7.other_ref), custom_call_target="tpu_custom_call" | custom-call | tf_op jit(solution)/shard_map/pallas_call | solution.py:196
  38.8 3.8 %all-to-all-start = ((f32[4,2,2,16,8,128]{5,4,3,2,1,0:T(8,128)}), f32[4,2,2,16,8,128]{5,4,3,2,1,0:T(8,128)S(1)}, u32[]{:S(2)}, u32[]{:S(2)}) async-start(f32[4,2,2,16,8,128]{5,4,3,2,1,0:T(8,128)} %shard_map.91), calls=%async_computation | async-start | bytes 2097152 | tf_op jit(solution)/shard_map/all_to_all | solution.py:203
  42.6 5.2 %collective-permute-start.5 = (f32[2,264,256]{2,1,0:T(8,128)S(1)}, f32[2,264,256]{2,1,0:T(8,128)S(1)}, u32[]{:S(2)}, u32[]{:S(2)}) collective-permute-start(f32[2,264,256]{2,1,0:T(8,128)S(1)} %get-tuple-element.17.grad_ref), channel_id=1, source_target_pairs={{0,1},{1,2},{2,3},{3,4},{4,5},{5,6},{6,7},{7,8},{8,9},{9,10},{10,1... | collective-permute-start | bytes 1622024 | tf_op jit(solution)/shard_map/ppermute | solution.py:22
  47.8 10.4 %all-to-all-done = f32[4,2,2,16,8,128]{5,4,3,2,1,0:T(8,128)S(1)} async-done(((f32[4,2,2,16,8,128]{5,4,3,2,1,0:T(8,128)}), f32[4,2,2,16,8,128]{5,4,3,2,1,0:T(8,128)S(1)}, u32[]{:S(2)}, u32[]{:S(2)}) %all-to-all-start) | async-done | bytes 1048608 | tf_op jit(solution)/shard_map/all_to_all | solution.py:203
  58.2 0.8 reduce_sum.18
  59.0 21.3 %all-to-all-start.1 = ((f32[64,8,128]{2,1,0:T(8,128)}), f32[64,8,128]{2,1,0:T(8,128)S(1)}, u32[]{:S(2)}, u32[]{:S(2)}) async-start(f32[64,8,128]{2,1,0:T(8,128)} %bitcast.6), calls=%async_computation.1 | async-start | bytes 524288 | tf_op jit(solution)/shard_map/all_to_all | solution.py:213
  80.3 0.0 collective-permute-done.5.left_ref
  80.3 0.8 shard_map.90
  81.1 1.9 %collective-permute-start.6 = (f32[2,256,256]{2,1,0:T(8,128)S(1)}, f32[2,256,256]{2,1,0:T(8,128)S(1)}, u32[]{:S(2)}, u32[]{:S(2)}) collective-permute-start(f32[2,256,256]{2,1,0:T(8,128)S(1)} %get-tuple-element.19), channel_id=1, source_target_pairs={{0,32},{32,64},{64,96},{96,128},{128,160},{160,192},{192,224},{224... | collective-permute-start | bytes 1572872 | tf_op jit(solution)/shard_map/ppermute | solution.py:22
  83.0 12.1 %collective-permute-done.6 = f32[2,256,256]{2,1,0:T(8,128)S(1)} collective-permute-done((f32[2,256,256]{2,1,0:T(8,128)S(1)}, f32[2,256,256]{2,1,0:T(8,128)S(1)}, u32[]{:S(2)}, u32[]{:S(2)}) %collective-permute-start.6) | collective-permute-done | bytes 524320 | tf_op jit(solution)/shard_map/ppermute | solution.py:22
  95.2 0.9 add.20
  96.0 4.6 %all-to-all-done.1 = f32[64,8,128]{2,1,0:T(8,128)S(1)} async-done(((f32[64,8,128]{2,1,0:T(8,128)}), f32[64,8,128]{2,1,0:T(8,128)S(1)}, u32[]{:S(2)}, u32[]{:S(2)}) %all-to-all-start.1) | async-done | bytes 262176 | tf_op jit(solution)/shard_map/all_to_all | solution.py:213
  100.6 0.1 reduce_sum.19
  100.7 0.1 reshape.15
  100.8 0.6 copy.10
Async XLA Ops:
  0.6 4.7 %copy-start.4 = (s32[1,1,1,2]{3,2,1,0:T(1,128)S(1)}, s32[1,1,1,2]{3,2,1,0:T(1,128)}, u32[]{:S(2)}) copy-start(s32[1,1,1,2]{3,2,1,0:T(1,128)} %param.10) | copy-start | bytes 28
  1.6 22.7 %copy-start = (bf16[4,2,256,256]{3,2,1,0:T(8,128)(2,1)S(1)}, bf16[4,2,256,256]{3,2,1,0:T(8,128)(2,1)}, u32[]{:S(2)}) copy-start(bf16[4,2,256,256]{3,2,1,0:T(8,128)(2,1)} %probe_in.1) | copy-start | bytes 3145732
  1.6 13.4 %collective-permute-start = (f32[2,144,256]{2,1,0:T(8,128)S(1)}, f32[2,144,256]{2,1,0:T(8,128)S(1)}, u32[]{:S(2)}, u32[]{:S(2)}) collective-permute-start(f32[2,144,256]{2,1,0:T(8,128)S(1)} %slice.9.own0_ref.own_ref), channel_id=1, source_target_pairs={{1,0},{2,1},{3,2},{4,3},{5,4},{6,5},{7,6},{8,7},{9,8},{10,9},{11,1... | collective-permute-start | bytes 884744 | tf_op jit(solution)/shard_map/ppermute | solution.py:22
  4.0 14.8 %collective-permute-start.1 = (f32[2,112,256]{2,1,0:T(8,128)S(1)}, f32[2,112,256]{2,1,0:T(8,128)S(1)}, u32[]{:S(2)}, u32[]{:S(2)}) collective-permute-start(f32[2,112,256]{2,1,0:T(8,128)S(1)} %slice.11.own1_ref.own_ref), channel_id=1, source_target_pairs={{1,0},{2,1},{3,2},{4,3},{5,4},{6,5},{7,6},{8,7},{9,8},{10,9},{11,1... | collective-permute-start | bytes 688136 | tf_op jit(solution)/shard_map/ppermute | solution.py:22
  5.4 7.0 %collective-permute-start.2 = (s32[2]{0:T(128)S(1)}, s32[2]{0:T(128)S(1)}, u32[]{:S(2)}, u32[]{:S(2)}) collective-permute-start(s32[2]{0:T(128)S(1)} %add_subtract_fusion), channel_id=1, source_target_pairs={{0,32},{32,64},{64,96},{96,128},{128,160},{160,192},{192,224},{224... | collective-permute-start | bytes 32 | tf_op jit(solution)/shard_map/ppermute | solution.py:22
  15.1 9.3 %copy-start.2 = (bf16[512,512]{1,0:T(8,128)(2,1)S(1)}, bf16[512,512]{1,0:T(8,128)(2,1)}, u32[]{:S(2)}) copy-start(bf16[512,512]{1,0:T(8,128)(2,1)} %constant.48.clone.ta_in) | copy-start | bytes 1572868
  15.6 8.7 %copy-start.1 = (bf16[512,512]{1,0:T(8,128)(2,1)S(1)}, bf16[512,512]{1,0:T(8,128)(2,1)}, u32[]{:S(2)}) copy-start(bf16[512,512]{1,0:T(8,128)(2,1)} %constant.49.clone.tb_in) | copy-start | bytes 1572868
  15.7 11.8 %collective-permute-start.3 = (f32[2,144,256]{2,1,0:T(8,128)S(1)}, f32[2,144,256]{2,1,0:T(8,128)}, u32[]{:S(2)}, u32[]{:S(2)}) collective-permute-start(f32[2,144,256]{2,1,0:T(8,128)S(1)} %shard_map.87), channel_id=1, source_target_pairs={{32,0},{64,32},{96,64},{128,96},{160,128},{192,160},{224,192},{256... | collective-permute-start | bytes 884744 | tf_op jit(solution)/shard_map/ppermute | solution.py:22
  20.1 7.4 %collective-permute-start.4 = (f32[2,112,256]{2,1,0:T(8,128)}, f32[2,112,256]{2,1,0:T(8,128)}, u32[]{:S(2)}, u32[]{:S(2)}) collective-permute-start(f32[2,112,256]{2,1,0:T(8,128)} %shard_map.88), channel_id=1, source_target_pairs={{32,0},{64,32},{96,64},{128,96},{160,128},{192,160},{224,192},{256... | collective-permute-start | bytes 688136 | tf_op jit(solution)/shard_map/ppermute | solution.py:22
  24.4 1.0 copy-start.3
  32.9 4.6 %collective-permute-start.7 = (f32[8,128,256]{2,1,0:T(8,128)S(1)}, f32[8,128,256]{2,1,0:T(8,128)S(1)}, u32[]{:S(2)}, u32[]{:S(2)}) collective-permute-start(f32[8,128,256]{2,1,0:T(8,128)S(1)} %get-tuple-element.21), channel_id=1, source_target_pairs={{0,32},{32,0},{1,33},{33,1},{2,34},{34,2},{3,35},{35,3},{4,36},{36... | collective-permute-start | bytes 3145736 | tf_op jit(solution)/shard_map/ppermute | solution.py:194
  38.8 19.4 %all-to-all-start = ((f32[4,2,2,16,8,128]{5,4,3,2,1,0:T(8,128)}), f32[4,2,2,16,8,128]{5,4,3,2,1,0:T(8,128)S(1)}, u32[]{:S(2)}, u32[]{:S(2)}) async-start(f32[4,2,2,16,8,128]{5,4,3,2,1,0:T(8,128)} %shard_map.91), calls=%async_computation | async-start | bytes 2097152 | tf_op jit(solution)/shard_map/all_to_all | solution.py:203
  42.6 37.7 %collective-permute-start.5 = (f32[2,264,256]{2,1,0:T(8,128)S(1)}, f32[2,264,256]{2,1,0:T(8,128)S(1)}, u32[]{:S(2)}, u32[]{:S(2)}) collective-permute-start(f32[2,264,256]{2,1,0:T(8,128)S(1)} %get-tuple-element.17.grad_ref), channel_id=1, source_target_pairs={{0,1},{1,2},{2,3},{3,4},{4,5},{5,6},{6,7},{7,8},{8,9},{9,10},{10,1... | collective-permute-start | bytes 1622024 | tf_op jit(solution)/shard_map/ppermute | solution.py:22
  59.0 41.6 %all-to-all-start.1 = ((f32[64,8,128]{2,1,0:T(8,128)}), f32[64,8,128]{2,1,0:T(8,128)S(1)}, u32[]{:S(2)}, u32[]{:S(2)}) async-start(f32[64,8,128]{2,1,0:T(8,128)} %bitcast.6), calls=%async_computation.1 | async-start | bytes 524288 | tf_op jit(solution)/shard_map/all_to_all | solution.py:213
  81.1 14.1 %collective-permute-start.6 = (f32[2,256,256]{2,1,0:T(8,128)S(1)}, f32[2,256,256]{2,1,0:T(8,128)S(1)}, u32[]{:S(2)}, u32[]{:S(2)}) collective-permute-start(f32[2,256,256]{2,1,0:T(8,128)S(1)} %get-tuple-element.19), channel_id=1, source_target_pairs={{0,32},{32,64},{64,96},{96,128},{128,160},{160,192},{192,224},{224... | collective-permute-start | bytes 1572872 | tf_op jit(solution)/shard_map/ppermute | solution.py:22

commit v3 on v2

--- a/solution.py
+++ b/solution.py
@@ -13,7 +13,6 @@
 
 ROW = ("ylo", "x", "core")
 COL = ("z", "yhi")
-FIRST_ROWS = 144
 
 
 def shifted(value, axis, steps):
@@ -31,17 +30,19 @@
     return np.block([[real, imag], [-imag, real]]), np.block([[real, -imag], [imag, real]])
 
 
-def mix_kernel(corner_ref, own_ref, right_ref, out_ref):
-    cols = lax.broadcasted_iota(jnp.int32, own_ref.shape, 2)
-    out_ref[...] = jnp.where(cols >= corner_ref[1], own_ref[...], right_ref[...])
-
-
-def side_kernel(scal_ref, own0_ref, own1_ref, right0_ref, right1_ref, probe_in, amp_in, ta_in, tb_in,
+def near_kernel(value_ref, out_ref):
+    out_ref[...] = value_ref[...]
+
+
+def mix_kernel(corner_ref, own_ref, below_ref, out_ref):
+    rows = lax.broadcasted_iota(jnp.int32, own_ref.shape, 1)
+    out_ref[...] = jnp.where(rows >= corner_ref[0], own_ref[...], below_ref[...])
+
+
+def side_kernel(scal_ref, own_ref, below_ref, probe_in, amp_in, ta_in, tb_in,
                 side_ref, probe_ref, amp_ref, ta_ref, tb_ref):
-    first = own0_ref.shape[1]
-    cols = lax.broadcasted_iota(jnp.int32, side_ref.shape, 2)
-    side_ref[:, :first] = jnp.where(cols[:, :first] >= scal_ref[1], own0_ref[...], right0_ref[...])
-    side_ref[:, first:] = jnp.where(cols[:, first:] >= scal_ref[1], own1_ref[...], right1_ref[...])
+    rows = lax.broadcasted_iota(jnp.int32, own_ref.shape, 1)
+    side_ref[...] = jnp.where(rows >= scal_ref[0], own_ref[...], below_ref[...])
     for src, dst in ((probe_in, probe_ref), (amp_in, amp_ref), (ta_in, ta_ref), (tb_in, tb_ref)):
         dst[...] = src[...]
 
@@ -70,17 +71,16 @@
 
 
 def patch_kernel(
-    inverse_slots, scal_ref, side_ref, under0_ref, under1_ref, probe_ref, amp_ref, ta_ref, tb_ref,
+    inverse_slots, scal_ref, side_ref, beside_ref, probe_ref, amp_ref, ta_ref, tb_ref,
     keep_ref, send_ref, grad_ref,
     patch_s, far_s, grad_s, mid_s,
 ):
     modes = probe_ref.shape[0]
     n = side_ref.shape[1]
     row0, col0, live, parity = scal_ref[0], scal_ref[1], scal_ref[2], scal_ref[3]
-    rows = lax.broadcasted_iota(jnp.int32, (n, n), 0)
+    cols = lax.broadcasted_iota(jnp.int32, (n, n), 1)
     for k in range(2):
-        under = jnp.concatenate([under0_ref[k], under1_ref[k]], 0)
-        mixed = jnp.where(rows >= row0, side_ref[k], under)
+        mixed = jnp.where(cols >= col0, side_ref[k], beside_ref[k])
         mixed = pltpu.roll(mixed, (n - row0) % n, 0)
         patch_s[k] = pltpu.roll(mixed, (n - col0) % n, 1)
     xr, xi = patch_s[0], patch_s[1]
@@ -145,22 +145,25 @@
     live = (counts[0, 0] > 0).astype(jnp.int32)
     row0, col0 = corner[0], corner[1]
 
-    own = [specimen[:, :FIRST_ROWS], lax.optimization_barrier(specimen)[:, FIRST_ROWS:]]
-    right = [shifted(part_rows, COL, -1) for part_rows in own]
     vmem = pl.BlockSpec(memory_space=pltpu.VMEM)
     smem = pl.BlockSpec(memory_space=pltpu.SMEM)
-    above_corner = shifted(corner, ROW, 1)
-    mixed = [
-        pl.pallas_call(
-            mix_kernel,
-            out_shape=jax.ShapeDtypeStruct(mine.shape, jnp.float32),
-            in_specs=[smem, vmem, vmem],
-            out_specs=vmem,
-            compiler_params=pltpu.CompilerParams(vmem_limit_bytes=2 << 20),
-        )(above_corner, mine, beside)
-        for mine, beside in zip(own, right)
-    ]
-    under = [shifted(part_rows, ROW, -1) for part_rows in mixed]
+    below = shifted(specimen, ROW, -1)
+    left_corner = shifted(corner, COL, 1)
+    own = pl.pallas_call(
+        near_kernel,
+        out_shape=jax.ShapeDtypeStruct(specimen.shape, jnp.float32),
+        in_specs=[vmem],
+        out_specs=vmem,
+        compiler_params=pltpu.CompilerParams(vmem_limit_bytes=3 << 20),
+    )(specimen)
+    mixed = pl.pallas_call(
+        mix_kernel,
+        out_shape=jax.ShapeDtypeStruct(specimen.shape, jnp.float32),
+        in_specs=[smem, vmem, vmem],
+        out_specs=vmem,
+        compiler_params=pltpu.CompilerParams(vmem_limit_bytes=3 << 20),
+    )(left_corner, own, below)
+    beside = shifted(mixed, COL, -1)
 
     scalars = jnp.stack([row0, col0, live, row_id % 2]).astype(jnp.int32)
     table_a, table_b = dft_tables(n)
@@ -169,10 +172,10 @@
         side_kernel,
         out_shape=(jax.ShapeDtypeStruct((2, n, n), jnp.float32),)
         + tuple(jax.ShapeDtypeStruct(value.shape, value.dtype) for value in operands),
-        in_specs=[smem] + [vmem] * 8,
+        in_specs=[smem] + [vmem] * 6,
         out_specs=(vmem,) * 5,
         compiler_params=pltpu.CompilerParams(vmem_limit_bytes=10 << 20),
-    )(scalars, *own, *right, *operands)
+    )(scalars, own, below, *operands)
     keep, send, grad = pl.pallas_call(
         functools.partial(patch_kernel, 1.0 / slots),
         out_shape=(
@@ -180,7 +183,7 @@
             jax.ShapeDtypeStruct((half, 2 * modes * part, n), jnp.float32),
             jax.ShapeDtypeStruct((2, n + 8, n), jnp.float32),
         ),
-        in_specs=[smem] + [vmem] * 7,
+        in_specs=[smem] + [vmem] * 6,
         out_specs=(vmem,) * 3,
         scratch_shapes=[
             pltpu.VMEM((2, n, n), jnp.float32),
@@ -189,7 +192,7 @@
             pltpu.VMEM((modes * n, 2 * n), jnp.bfloat16),
         ],
         compiler_params=pltpu.CompilerParams(vmem_limit_bytes=14 << 20),
-    )(scalars, side, *under, *operands)
+    )(scalars, side, beside, *operands)
 
     other = lax.ppermute(send, "core", [(0, 1), (1, 0)])
     from_left = shifted(grad, COL, 1)

time: 102 us -> 102 us (level)
  waiting for transfers between devices: 39.8 us -> 42.6 us
  starting transfers between devices: 44.5 us -> 43.1 us
  Pallas kernels: 10.1 us -> 8.72 us
    ppermute x7 -> x5, waiting for transfers between devices: 22.3 us -> 25.8 us  [shifted(): lax.ppermute(value, axis, [(source, source + steps) for source in range(f...]
    slice x2 -> x0, local copies, waits for them, and re-layouts: 1.95 us -> none  [the longest x1 0.99 us: shards(): specimen[:, :FIRST_ROWS]]
    unnamed x11 -> x13, local copies, waits for them, and re-layouts: 1.59 us -> 3.36 us
    pallas_call x2, Pallas kernels: 1.82 us -> 0.63 us  [the longest x1 0.59 us: shards(): pl.pallas_call(mix_kernel, out_shape=jax.ShapeDtypeStruct(specimen.shape,...]
    all_to_all x1, starting transfers between devices: 21.3 us -> 20.1 us  [shards(): lax.all_to_all(summed, ('yhi', 'ylo', 'z'), 0, 0, tiled=True).sum(0)]
    ppermute x7 -> x5, starting transfers between devices: 17.4 us -> 17.5 us  [shifted(): lax.ppermute(value, axis, [(source, source + steps) for source in range(f...]
  transfers between devices with their start and end apart: 10 -> 8, of which waited for: 8 -> 7; matrix products, arithmetic and copies ran while one was open for 3% -> 2% of each run, Pallas kernels for 3% -> 2%
where the time goes in v3:
time: 102 us; the launch traced here: 101 us
  starting transfers between devices  43.1 us (42%)
  waiting for transfers between devices  42.6 us (42%)
  Pallas kernels  8.72 us (9%)
  local copies, waits for them, and re-layouts  3.46 us (3%)
  other arithmetic  1.84 us (2%)
  between operations  1.47 us (1%)
    ppermute x5, waiting for transfers between devices, shifted(): lax.ppermute(value, axis, [(source, source + steps) for source in range(f...  25.8 us
    all_to_all x1, starting transfers between devices, shards(): lax.all_to_all(summed, ('yhi', 'ylo', 'z'), 0, 0, tiled=True).sum(0)  20.1 us
    ppermute x5, starting transfers between devices, shifted(): lax.ppermute(value, axis, [(source, source + steps) for source in range(f...  17.5 us
    all_to_all x1, waiting for transfers between devices, shards(): summed = lax.all_to_all(summed, 'x', 0, 0, tiled=True)  9.78 us
    pallas_call x1, Pallas kernels, shards(): pl.pallas_call(functools.partial(patch_kernel, 1.0 / slots), out_shape=(j...  5.26 us
    all_to_all x1, waiting for transfers between devices, shards(): lax.all_to_all(summed, ('yhi', 'ylo', 'z'), 0, 0, tiled=True).sum(0)  4.39 us
    all_to_all x1, starting transfers between devices, shards(): summed = lax.all_to_all(summed, 'x', 0, 0, tiled=True)  3.51 us
    unnamed x13, local copies, waits for them, and re-layouts  3.36 us
  transfers between devices with their start and end apart: 8, of which 7 were waited for; matrix products, arithmetic and copies ran while one was open for 2% of the time, Pallas kernels for 2%

profile of v3, /device:TPU:8, one launch (start us, length us, event | category | flops | bytes accessed | tf_op | source)
XLA Modules:
  0.0 101.2 jit_solution(14344791257605659056)
XLA Ops:
  0.6 4.0 %collective-permute-start = (f32[2,256,256]{2,1,0:T(8,128)}, f32[2,256,256]{2,1,0:T(8,128)S(1)}, u32[]{:S(2)}, u32[]{:S(2)}) collective-permute-start(f32[2,256,256]{2,1,0:T(8,128)} %value_ref.1), channel_id=1, source_target_pairs={{32,0},{64,32},{96,64},{128,96},{160,128},{192,160},{224,192},{256... | collective-permute-start | bytes 1572872 | tf_op jit(solution)/shard_map/ppermute | solution.py:21
  4.6 0.0 copy-start.5
  4.7 0.6 copy-done.5
  5.3 0.1 add_subtract_fusion
  5.4 4.5 %collective-permute-start.1 = (s32[2]{0:T(128)S(1)}, s32[2]{0:T(128)S(1)}, u32[]{:S(2)}, u32[]{:S(2)}) collective-permute-start(s32[2]{0:T(128)S(1)} %add_subtract_fusion), channel_id=1, source_target_pairs={{0,1},{1,2},{2,3},{3,4},{4,5},{5,6},{6,7},{7,8},{8,9},{9,10},{10,1... | collective-permute-start | bytes 32 | tf_op jit(solution)/shard_map/ppermute | solution.py:21
  9.9 0.0 copy-start.1
  9.9 1.0 %copy-done.1 = f32[2,256,256]{2,1,0:T(8,128)S(1)} copy-done((f32[2,256,256]{2,1,0:T(8,128)S(1)}, f32[2,256,256]{2,1,0:T(8,128)}, u32[]{:S(2)}) %copy-start.1) | copy-done | bytes 524312
  10.9 0.0 copy-start.4
  11.0 0.0 copy-start
  11.0 0.0 copy-start.2
  11.0 0.2 collective-permute-done.1.corner_ref
  11.1 0.5 collective-permute-done.below_ref
  11.6 0.6 shard_map.88
  12.2 1.3 %collective-permute-start.2 = (f32[2,256,256]{2,1,0:T(8,128)S(1)}, f32[2,256,256]{2,1,0:T(8,128)}, u32[]{:S(2)}, u32[]{:S(2)}) collective-permute-start(f32[2,256,256]{2,1,0:T(8,128)S(1)} %shard_map.88), channel_id=1, source_target_pairs={{1,0},{2,1},{3,2},{4,3},{5,4},{6,5},{7,6},{8,7},{9,8},{10,9},{11,1... | collective-permute-start | bytes 1572872 | tf_op jit(solution)/shard_map/ppermute | solution.py:21
  14.2 0.1 pad_add_fusion.scal_ref
  14.3 0.0 copy-done.4
  14.3 0.0 copy-done
  14.3 0.0 copy-done.2
  14.3 0.0 copy-start.3
  14.3 1.0 %copy-done.3 = bf16[512,512]{1,0:T(8,128)(2,1)S(1)} copy-done((bf16[512,512]{1,0:T(8,128)(2,1)S(1)}, bf16[512,512]{1,0:T(8,128)(2,1)}, u32[]{:S(2)}) %copy-start.3) | copy-done | bytes 524312
  15.3 0.7 shard_map.87
  16.1 13.1 %collective-permute-done.2.beside_ref = f32[2,256,256]{2,1,0:T(8,128)} collective-permute-done((f32[2,256,256]{2,1,0:T(8,128)S(1)}, f32[2,256,256]{2,1,0:T(8,128)}, u32[]{:S(2)}, u32[]{:S(2)}) %collective-permute-start.2) | collective-permute-done | bytes 524320 | tf_op jit(solution)/shard_map/ppermute | solution.py:21
  29.2 5.3 %shard_map.89 = (f32[8,128,256]{2,1,0:T(8,128)S(1)}, f32[8,128,256]{2,1,0:T(8,128)S(1)}, f32[2,264,256]{2,1,0:T(8,128)S(1)}) custom-call(s32[4]{0:T(128)S(1)} %pad_add_fusion.scal_ref, f32[2,256,256]{2,1,0:T(8,128)S(1)} %get-tuple-element.12.side_ref, f32[2,256,256]{2,1,0:T(8,128)} %collective-permute-done.2.beside_ref, ...), custom_call_target="tpu_custom_call" | custom-call | tf_op jit(solution)/shard_map/pallas_call | solution.py:179
  34.4 1.9 %collective-permute-start.5 = (f32[8,128,256]{2,1,0:T(8,128)S(1)}, f32[8,128,256]{2,1,0:T(8,128)S(1)}, u32[]{:S(2)}, u32[]{:S(2)}) collective-permute-start(f32[8,128,256]{2,1,0:T(8,128)S(1)} %get-tuple-element.21), channel_id=1, source_target_pairs={{0,32},{32,0},{1,33},{33,1},{2,34},{34,2},{3,35},{35,3},{4,36},{36... | collective-permute-start | bytes 3145736 | tf_op jit(solution)/shard_map/ppermute | solution.py:197
  36.3 2.6 %collective-permute-done.5.other_ref = f32[8,128,256]{2,1,0:T(8,128)S(1)} collective-permute-done((f32[8,128,256]{2,1,0:T(8,128)S(1)}, f32[8,128,256]{2,1,0:T(8,128)S(1)}, u32[]{:S(2)}, u32[]{:S(2)}) %collective-permute-start.5) | collective-permute-done | bytes 1048608 | tf_op jit(solution)/shard_map/ppermute | solution.py:197
  39.0 1.3 %shard_map.91 = f32[4,2,2,16,8,128]{5,4,3,2,1,0:T(8,128)} custom-call(f32[8,128,256]{2,1,0:T(8,128)S(1)} %get-tuple-element.20.keep_ref, f32[8,128,256]{2,1,0:T(8,128)S(1)} %collective-permute-done.5.other_ref), custom_call_target="tpu_custom_call" | custom-call | tf_op jit(solution)/shard_map/pallas_call | solution.py:199
  40.3 3.5 %all-to-all-start = ((f32[4,2,2,16,8,128]{5,4,3,2,1,0:T(8,128)}), f32[4,2,2,16,8,128]{5,4,3,2,1,0:T(8,128)S(1)}, u32[]{:S(2)}, u32[]{:S(2)}) async-start(f32[4,2,2,16,8,128]{5,4,3,2,1,0:T(8,128)} %shard_map.91), calls=%async_computation | async-start | bytes 2097152 | tf_op jit(solution)/shard_map/all_to_all | solution.py:206
  43.8 5.9 %collective-permute-start.3 = (f32[2,264,256]{2,1,0:T(8,128)S(1)}, f32[2,264,256]{2,1,0:T(8,128)S(1)}, u32[]{:S(2)}, u32[]{:S(2)}) collective-permute-start(f32[2,264,256]{2,1,0:T(8,128)S(1)} %get-tuple-element.17.grad_ref), channel_id=1, source_target_pairs={{0,1},{1,2},{2,3},{3,4},{4,5},{5,6},{6,7},{7,8},{8,9},{9,10},{10,1... | collective-permute-start | bytes 1622024 | tf_op jit(solution)/shard_map/ppermute | solution.py:21
  49.7 9.8 %all-to-all-done = f32[4,2,2,16,8,128]{5,4,3,2,1,0:T(8,128)S(1)} async-done(((f32[4,2,2,16,8,128]{5,4,3,2,1,0:T(8,128)}), f32[4,2,2,16,8,128]{5,4,3,2,1,0:T(8,128)S(1)}, u32[]{:S(2)}, u32[]{:S(2)}) %all-to-all-start) | async-done | bytes 1048608 | tf_op jit(solution)/shard_map/all_to_all | solution.py:206
  59.5 0.8 reduce_sum.18
  60.2 20.1 %all-to-all-start.1 = ((f32[64,8,128]{2,1,0:T(8,128)}), f32[64,8,128]{2,1,0:T(8,128)S(1)}, u32[]{:S(2)}, u32[]{:S(2)}) async-start(f32[64,8,128]{2,1,0:T(8,128)} %bitcast.6), calls=%async_computation.1 | async-start | bytes 524288 | tf_op jit(solution)/shard_map/all_to_all | solution.py:216
  80.3 0.0 collective-permute-done.3.left_ref
  80.4 0.8 shard_map.90
  81.1 1.9 %collective-permute-start.4 = (f32[2,256,256]{2,1,0:T(8,128)S(1)}, f32[2,256,256]{2,1,0:T(8,128)S(1)}, u32[]{:S(2)}, u32[]{:S(2)}) collective-permute-start(f32[2,256,256]{2,1,0:T(8,128)S(1)} %get-tuple-element.19), channel_id=1, source_target_pairs={{0,32},{32,64},{64,96},{96,128},{128,160},{160,192},{192,224},{224... | collective-permute-start | bytes 1572872 | tf_op jit(solution)/shard_map/ppermute | solution.py:21
  83.1 12.1 %collective-permute-done.4 = f32[2,256,256]{2,1,0:T(8,128)S(1)} collective-permute-done((f32[2,256,256]{2,1,0:T(8,128)S(1)}, f32[2,256,256]{2,1,0:T(8,128)S(1)}, u32[]{:S(2)}, u32[]{:S(2)}) %collective-permute-start.4) | collective-permute-done | bytes 524320 | tf_op jit(solution)/shard_map/ppermute | solution.py:21
  95.1 0.9 add.20
  96.0 4.4 %all-to-all-done.1 = f32[64,8,128]{2,1,0:T(8,128)S(1)} async-done(((f32[64,8,128]{2,1,0:T(8,128)}), f32[64,8,128]{2,1,0:T(8,128)S(1)}, u32[]{:S(2)}, u32[]{:S(2)}) %all-to-all-start.1) | async-done | bytes 262176 | tf_op jit(solution)/shard_map/all_to_all | solution.py:216
  100.4 0.1 reduce_sum.19
  100.5 0.1 reshape.15
  100.6 0.6 copy.10
  (1 shorter events, 0.0 us)
Async XLA Ops:
  0.6 11.0 %collective-permute-start = (f32[2,256,256]{2,1,0:T(8,128)}, f32[2,256,256]{2,1,0:T(8,128)S(1)}, u32[]{:S(2)}, u32[]{:S(2)}) collective-permute-start(f32[2,256,256]{2,1,0:T(8,128)} %value_ref.1), channel_id=1, source_target_pairs={{32,0},{64,32},{96,64},{128,96},{160,128},{192,160},{224,192},{256... | collective-permute-start | bytes 1572872 | tf_op jit(solution)/shard_map/ppermute | solution.py:21
  4.6 0.7 copy-start.5
  5.4 5.8 %collective-permute-start.1 = (s32[2]{0:T(128)S(1)}, s32[2]{0:T(128)S(1)}, u32[]{:S(2)}, u32[]{:S(2)}) collective-permute-start(s32[2]{0:T(128)S(1)} %add_subtract_fusion), channel_id=1, source_target_pairs={{0,1},{1,2},{2,3},{3,4},{4,5},{5,6},{6,7},{7,8},{8,9},{9,10},{10,1... | collective-permute-start | bytes 32 | tf_op jit(solution)/shard_map/ppermute | solution.py:21
  9.9 1.0 %copy-start.1 = (f32[2,256,256]{2,1,0:T(8,128)S(1)}, f32[2,256,256]{2,1,0:T(8,128)}, u32[]{:S(2)}) copy-start(f32[2,256,256]{2,1,0:T(8,128)} %value_ref.1) | copy-start | bytes 1572868
  10.9 3.4 %copy-start.4 = (f32[1,1,1,256,256]{4,3,2,1,0:T(8,128)S(1)}, f32[1,1,1,256,256]{4,3,2,1,0:T(8,128)}, u32[]{:S(2)}) copy-start(f32[1,1,1,256,256]{4,3,2,1,0:T(8,128)} %param.9) | copy-start | bytes 786436
  11.0 3.3 %copy-start = (bf16[4,2,256,256]{3,2,1,0:T(8,128)(2,1)S(1)}, bf16[4,2,256,256]{3,2,1,0:T(8,128)(2,1)}, u32[]{:S(2)}) copy-start(bf16[4,2,256,256]{3,2,1,0:T(8,128)(2,1)} %probe_in.1) | copy-start | bytes 3145732
  11.0 3.3 %copy-start.2 = (bf16[512,512]{1,0:T(8,128)(2,1)S(1)}, bf16[512,512]{1,0:T(8,128)(2,1)}, u32[]{:S(2)}) copy-start(bf16[512,512]{1,0:T(8,128)(2,1)} %constant.49.clone.tb_in) | copy-start | bytes 1572868
  12.2 16.9 %collective-permute-start.2 = (f32[2,256,256]{2,1,0:T(8,128)S(1)}, f32[2,256,256]{2,1,0:T(8,128)}, u32[]{:S(2)}, u32[]{:S(2)}) collective-permute-start(f32[2,256,256]{2,1,0:T(8,128)S(1)} %shard_map.88), channel_id=1, source_target_pairs={{1,0},{2,1},{3,2},{4,3},{5,4},{6,5},{7,6},{8,7},{9,8},{10,9},{11,1... | collective-permute-start | bytes 1572872 | tf_op jit(solution)/shard_map/ppermute | solution.py:21
  14.3 1.0 %copy-start.3 = (bf16[512,512]{1,0:T(8,128)(2,1)S(1)}, bf16[512,512]{1,0:T(8,128)(2,1)}, u32[]{:S(2)}) copy-start(bf16[512,512]{1,0:T(8,128)(2,1)} %constant.48.clone.ta_in) | copy-start | bytes 1572868
  34.4 4.6 %collective-permute-start.5 = (f32[8,128,256]{2,1,0:T(8,128)S(1)}, f32[8,128,256]{2,1,0:T(8,128)S(1)}, u32[]{:S(2)}, u32[]{:S(2)}) collective-permute-start(f32[8,128,256]{2,1,0:T(8,128)S(1)} %get-tuple-element.21), channel_id=1, source_target_pairs={{0,32},{32,0},{1,33},{33,1},{2,34},{34,2},{3,35},{35,3},{4,36},{36... | collective-permute-start | bytes 3145736 | tf_op jit(solution)/shard_map/ppermute | solution.py:197
  40.3 19.2 %all-to-all-start = ((f32[4,2,2,16,8,128]{5,4,3,2,1,0:T(8,128)}), f32[4,2,2,16,8,128]{5,4,3,2,1,0:T(8,128)S(1)}, u32[]{:S(2)}, u32[]{:S(2)}) async-start(f32[4,2,2,16,8,128]{5,4,3,2,1,0:T(8,128)} %shard_map.91), calls=%async_computation | async-start | bytes 2097152 | tf_op jit(solution)/shard_map/all_to_all | solution.py:206
  43.8 36.5 %collective-permute-start.3 = (f32[2,264,256]{2,1,0:T(8,128)S(1)}, f32[2,264,256]{2,1,0:T(8,128)S(1)}, u32[]{:S(2)}, u32[]{:S(2)}) collective-permute-start(f32[2,264,256]{2,1,0:T(8,128)S(1)} %get-tuple-element.17.grad_ref), channel_id=1, source_target_pairs={{0,1},{1,2},{2,3},{3,4},{4,5},{5,6},{6,7},{7,8},{8,9},{9,10},{10,1... | collective-permute-start | bytes 1622024 | tf_op jit(solution)/shard_map/ppermute | solution.py:21
  60.2 40.2 %all-to-all-start.1 = ((f32[64,8,128]{2,1,0:T(8,128)}), f32[64,8,128]{2,1,0:T(8,128)S(1)}, u32[]{:S(2)}, u32[]{:S(2)}) async-start(f32[64,8,128]{2,1,0:T(8,128)} %bitcast.6), calls=%async_computation.1 | async-start | bytes 524288 | tf_op jit(solution)/shard_map/all_to_all | solution.py:216
  81.1 14.0 %collective-permute-start.4 = (f32[2,256,256]{2,1,0:T(8,128)S(1)}, f32[2,256,256]{2,1,0:T(8,128)S(1)}, u32[]{:S(2)}, u32[]{:S(2)}) collective-permute-start(f32[2,256,256]{2,1,0:T(8,128)S(1)} %get-tuple-element.19), channel_id=1, source_target_pairs={{0,32},{32,64},{64,96},{96,128},{128,160},{160,192},{192,224},{224... | collective-permute-start | bytes 1572872 | tf_op jit(solution)/shard_map/ppermute | solution.py:21
